TPU v7x, 256 devices: a whole 4x4x8 slice. The times are simulated.
256 devices in a mesh: seq: 8 (over x, z_hi), head: 32 (over z_lo, y, core).
Axes of the slice: x: 4, y: 4, z: 8 (z_hi: 2, z_lo: 4; z = z_hi * 4 + z_lo), core: 2. Of those that a mesh axis runs over, the one named last changes fastest.
Arguments:
- tokens: bfloat16 [8192, 8192], P(('seq', 'head')), may hold values from -6 to 6
- in_x_weight: bfloat16 [8192, 10240], P(None, 'head'), may hold values from -0.0625 to 0.0625
- in_z_weight: bfloat16 [8192, 10240], P(None, 'head'), may hold values from -0.0625 to 0.0625
- in_bc_weight: bfloat16 [8192, 2048], P(None, 'head'), may hold values from -0.0625 to 0.0625
- in_dt_weight: bfloat16 [8192, 160], P(None, 'head'), may hold values from -0.0625 to 0.0625
- conv_x_weight: float32 [4, 10240], P(None, 'head'), may hold values from -3 to 3
- conv_bc_weight: float32 [4, 2048], P(None, 'head'), may hold values from -3 to 3
- dt_bias: float32 [160], P('head'), may hold values from -1 to 1
- a_log: float32 [160], P('head'), may hold values from -10 to -3.5
- skip_weight: float32 [160], P('head'), may hold values from 0.5 to 2
- norm_gain: float32 [10240], replicated, may hold values from 0.5 to 1.5
Outputs:
- mixed: bfloat16 [8192, 10240], P(('seq', 'head'))
All inputs are finite; a program needn't handle non-finite values.
Results may differ from a plain program's by a relative error of at most 0.013.
Values may be sent and summed in bfloat16 or wider, within the bound.
A program may use at most 128 MiB of HBM per device.

v0:
```python
import jax
import jax.numpy as jnp
from jax import lax
from jax.sharding import PartitionSpec as P

HEAD_DIM = 64
STATE = 128
GROUPS = 8
NORM_GROUP = 2048
SPAN = 128
CONV = 4


def passed_along(value, axis, steps):
    count = lax.axis_size(axis)
    leading, last = (max(0, -steps), min(count, count - steps))
    return lax.ppermute(value, axis, [(source, source + steps) for source in range(leading, last)])


def swapped(value, axis, apart):
    mask = 2**apart
    pairs = [(source, source ^ mask) for source in range(lax.axis_size(axis))]
    return lax.ppermute(value, axis, pairs)


def causal_conv(pre, tail, taps):
    padded = jnp.concatenate([tail.astype(jnp.float32), pre.astype(jnp.float32)], axis=0)
    total = jnp.zeros(pre.shape, jnp.float32)
    for k in range(CONV):
        total = total + taps[k][None, :] * padded[k : k + pre.shape[0]]
    return jax.nn.silu(total).astype(jnp.bfloat16)


def shards(
    tokens,
    in_x_weight,
    in_z_weight,
    in_bc_weight,
    in_dt_weight,
    conv_x_weight,
    conv_bc_weight,
    dt_bias,
    a_log,
    skip_weight,
    norm_gain,
):
    high = lax.Precision.HIGHEST
    width_x = in_x_weight.shape[1]
    width_bc = in_bc_weight.shape[1]
    heads_here = in_dt_weight.shape[1]
    piece = lax.all_gather(tokens, "head", axis=0, tiled=True)
    projected = jnp.concatenate(
        [
            jnp.dot(piece, in_x_weight, preferred_element_type=jnp.float32),
            jnp.dot(piece, in_z_weight, preferred_element_type=jnp.float32),
            jnp.dot(piece, in_bc_weight, preferred_element_type=jnp.float32),
            jnp.dot(piece, in_dt_weight, preferred_element_type=jnp.float32),
        ],
        axis=1,
    )
    x_pre = projected[:, :width_x].astype(jnp.bfloat16)
    z_gate = projected[:, width_x : 2 * width_x].astype(jnp.bfloat16)
    bc_pre = projected[:, 2 * width_x : 2 * width_x + width_bc].astype(jnp.bfloat16)
    dt_raw = projected[:, 2 * width_x + width_bc :]
    rows = x_pre.shape[0]
    tails = passed_along((x_pre[rows - CONV + 1 :], bc_pre[rows - CONV + 1 :]), "seq", 1)
    x_conv = causal_conv(x_pre, tails[0], conv_x_weight)
    bc_conv = causal_conv(bc_pre, tails[1], conv_bc_weight)
    in_group = lax.axis_size("head") // GROUPS
    collected = bc_conv
    position = lax.axis_index("head")
    for bit in range(in_group.bit_length() - 1):
        other = swapped(collected, "head", bit)
        upper = position >> bit & 1 == 1
        collected = jnp.where(
            upper,
            jnp.concatenate([other, collected], axis=1),
            jnp.concatenate([collected, other], axis=1),
        )
    step_size = jax.nn.softplus(dt_raw + dt_bias[None, :])
    decay = -step_size * jnp.exp(a_log)[None, :]
    blocks = rows // SPAN
    xs = x_conv.astype(jnp.float32).reshape(blocks, SPAN, heads_here, HEAD_DIM)
    bcs = collected.astype(jnp.float32).reshape(blocks, SPAN, 2 * STATE)
    decays = decay.reshape(blocks, SPAN, heads_here)
    steps_all = step_size.reshape(blocks, SPAN, heads_here)
    lower = jnp.arange(SPAN)[:, None] >= jnp.arange(SPAN)[None, :]

    def advance(carry, inputs):
        state, offset = carry
        xq, bcq, dq, sq = inputs
        bq = bcq[:, :STATE]
        cq = bcq[:, STATE:]
        cum = jnp.cumsum(dq, axis=0)
        diff = cum[:, None, :] - cum[None, :, :]
        lmat = jnp.exp(jnp.where(lower[:, :, None], diff, -jnp.inf))
        scores = jnp.dot(cq, bq.T, precision=high)
        mixing = lmat * scores[:, :, None]
        inputs_u = xq * sq[:, :, None]
        y_in = jnp.einsum("ijh,jhp->ihp", mixing, inputs_u, precision=high)
        y_st = jnp.einsum("in,hpn->ihp", cq, state, precision=high) * jnp.exp(cum)[:, :, None]
        tail = jnp.exp(cum[-1][None, :] - cum)
        fresh = jnp.einsum("jhp,jn->hpn", inputs_u * tail[:, :, None], bq, precision=high)
        new_state = state * jnp.exp(cum[-1])[:, None, None] + fresh
        return ((new_state, offset + cum[-1]), (y_in + y_st, cum + offset[None, :]))

    start = (
        jnp.zeros((heads_here, HEAD_DIM, STATE), jnp.float32),
        jnp.zeros((heads_here,), jnp.float32),
    )
    (local_state, total_log), (y_local, cum_all) = lax.scan(
        advance, start, (xs, bcs, decays, steps_all)
    )
    total_decay = jnp.exp(total_log)

    def relay(count, carried):
        return passed_along(total_decay[:, None, None] * carried + local_state, "seq", 1)

    incoming = lax.fori_loop(
        0, lax.axis_size("seq") - 1, relay, jnp.zeros((heads_here, HEAD_DIM, STATE), jnp.float32)
    )
    c_all = bcs[:, :, STATE:].reshape(rows, STATE)
    cum_flat = cum_all.reshape(rows, heads_here)
    carried_in = (
        jnp.einsum("in,hpn->ihp", c_all, incoming, precision=high) * jnp.exp(cum_flat)[:, :, None]
    )
    x_flat = xs.reshape(rows, heads_here, HEAD_DIM)
    y_total = (
        y_local.reshape(rows, heads_here, HEAD_DIM)
        + carried_in
        + skip_weight[None, :, None] * x_flat
    )
    y_ssd = y_total.reshape(rows, width_x).astype(jnp.bfloat16)
    y_back, z_back = (
        lax.all_to_all(y_ssd, "head", split_axis=0, concat_axis=1, tiled=True),
        lax.all_to_all(z_gate, "head", split_axis=0, concat_axis=1, tiled=True),
    )
    gated = y_back.astype(jnp.float32) * jax.nn.silu(z_back.astype(jnp.float32))
    mine = gated.shape[0]
    grouped = gated.reshape(mine, gated.shape[1] // NORM_GROUP, NORM_GROUP)
    scale = lax.rsqrt(jnp.mean(grouped * grouped, axis=2, keepdims=True) + 1e-05)
    mixed = (grouped * scale).reshape(mine, gated.shape[1]) * norm_gain[None, :]
    return mixed.astype(jnp.bfloat16)


def solution(mesh):
    placed = (
        P(("seq", "head"), None),
        P(None, "head"),
        P(None, "head"),
        P(None, "head"),
        P(None, "head"),
        P(None, "head"),
        P(None, "head"),
        P("head"),
        P("head"),
        P("head"),
        P(),
    )
    return jax.shard_map(
        shards, mesh=mesh, in_specs=placed, out_specs=P(("seq", "head"), None), check_vma=False
    )
```

profile of v0, /device:TPU:7, one launch (start us, length us, event | category | flops | bytes accessed | tf_op | source)
XLA Modules:
  0.0 427.5 jit_solution(9826043613374625098)
XLA Ops:
  9.7 102.6 %all-gather.2.cloned.1.call-done = bf16[1024,8192]{1,0:T(8,128)(2,1)} async-done(((bf16[32,8192]{1,0:T(8,128)(2,1)}), bf16[1024,8192]{1,0:T(8,128)(2,1)}) %all-gather.2.cloned.1.call-update) | async-done | bytes 16777232 | tf_op jit(solution)/shard_map/all_gather | solution.py:51
  112.3 11.1 %fusion.56 = (f32[1024,64]{0,1:T(8,128)S(1)}, bf16[1024,64]{0,1:T(8,128)(2,1)S(1)}) fusion(bf16[1024,8192]{1,0:T(8,128)(2,1)} %all-gather.2.cloned.1.call-done, bf16[8192,64]{0,1:T(8,128)(2,1)S(1)} %copy-done), kind=kOutput, calls=%fused_computation.103 | convolution fusion | flops 1073872896 | bytes 18219008 | tf_op jit(solution)/shard_map/dot_general | solution.py:56
  123.5 7.5 %collective-permute-start.2 = (bf16[3,64]{0,1:T(8,128)(2,1)S(1)}, bf16[3,64]{0,1:T(8,128)(2,1)S(1)}, u32[]{:S(2)}, u32[]{:S(2)}) collective-permute-start(bf16[3,64]{0,1:T(8,128)(2,1)S(1)} %slice.90), channel_id=1, source_target_pairs={{0,32},{32,64},{64,96},{96,128},{128,160},{160,192},{192,224},{1,3... | collective-permute-start | bytes 1160 | tf_op jit(solution)/shard_map/ppermute | solution.py:17
  131.0 14.0 %fusion.55 = (f32[1024,320]{0,1:T(8,128)}, bf16[1024,320]{0,1:T(8,128)(2,1)S(1)}) fusion(bf16[1024,8192]{1,0:T(8,128)(2,1)S(1)} %copy-done.2, bf16[8192,320]{0,1:T(8,128)(2,1)} %param.16), kind=kOutput, calls=%fused_computation.102 | convolution fusion | flops 5369364480 | bytes 23986176 | tf_op jit(solution)/shard_map/dot_general | solution.py:54
  145.1 2.2 collective-permute-start.1
  147.4 5.6 %convolution_convert_fusion = bf16[1024,320]{0,1:T(8,128)(2,1)S(1)} fusion(bf16[1024,8192]{1,0:T(8,128)(2,1)S(1)} %copy-done.2, bf16[8192,320]{0,1:T(8,128)(2,1)S(1)} %bitcast.114), kind=kOutput, calls=%fused_computation.56 | convolution fusion | flops 5369036800 | bytes 22675456 | tf_op jit(solution)/shard_map/dot_general | solution.py:55
  154.0 4.4 %negate_multiply_fusion = (f32[1024,5]{0,1:T(8,128)S(1)}, f32[1024,5]{0,1:T(8,128)S(1)}) fusion(f32[5]{0:T(128)S(1)} %exp.61, f32[5]{0:T(128)S(1)} %copy-done.7, bf16[1024,8192]{1,0:T(8,128)(2,1)S(1)} %copy-done.2, bf16[8192,5]{0,1:T(8,128)(2,1)S(1)} %copy-done.5), kind=kOutput, calls=%fused_computation.90 | convolution fusion | flops 83932160 | bytes 16900136 | tf_op jit(solution)/shard_map/dot_general | solution.py:57
  159.8 4.7 %all-to-all-start.1 = ((bf16[32,32,320]{2,1,0:T(8,128)(2,1)}), bf16[32,32,320]{2,1,0:T(8,128)(2,1)}, u32[]{:S(2)}, u32[]{:S(2)}) async-start(bf16[32,32,320]{2,1,0:T(8,128)(2,1)} %bitcast.11), calls=%async_computation.1 | async-start | bytes 1572864 | tf_op jit(solution)/shard_map/all_to_all | solution.py:136
  164.8 1.7 collective-permute-start.4
  166.5 4.4 %fusion.44 = f32[1024,320]{0,1:T(8,128)S(1)} fusion(f32[1024,320]{0,1:T(8,128)} %get-tuple-element.189, f32[320]{0:T(512)S(1)} %get-tuple-element.148, f32[3,320]{0,1:T(8,128)S(1)} %convert_element_type.79, f32[320]{0:T(512)S(1)} %get-tuple-element.149, f32[320]{0:T(512)S(1)} %get-tuple-element.147, f32[320]{0:T(512)S(1)} %get-tuple-element.146), kind=kLoop, calls=%fused_computation.71 | loop fusion | flops 5242880 | bytes 2630400 | tf_op jit(solution)/shard_map/convert_element_type | solution.py:83
  172.7 6.9 %collective-permute-done.4 = bf16[1024,128]{0,1:T(8,128)(2,1)} collective-permute-done((bf16[1024,128]{0,1:T(8,128)(2,1)S(1)}, bf16[1024,128]{0,1:T(8,128)(2,1)}, u32[]{:S(2)}, u32[]{:S(2)}) %collective-permute-start.4) | collective-permute-done | bytes 262176 | tf_op jit(solution)/shard_map/ppermute | solution.py:23
  181.9 85.7 %while.28 = (s32[]{:T(128)}, f32[5,64,128]{2,1,0:T(8,128)S(1)}, f32[5]{0:T(128)S(1)}, f32[8,128,5,64]{1,0,3,2:T(8,128)}, f32[8,128,5]{2,1,0:T(8,128)}, /*index=5...) while((s32[]{:T(128)}, f32[5,64,128]{2,1,0:T(8,128)S(1)}, ...), condition=%wide.region_2.3_spmd.clone, body=%wide.region_0.2_spmd.clone.sunk | while | flops 214622864 | bytes 2778969 | solution.py:111
  184.0 1.4 constant_dynamic-slice_fusion.2
  187.2 5.5 %dynamic_update_slice.14 = f32[8,128,5,64]{1,0,3,2:T(8,128)} dynamic-update-slice(f32[8,128,5,64]{1,0,3,2:T(8,128)} %get-tuple-element.298, f32[1,128,5,64]{1,0,3,2:T(1,128)S(1)} %bitcast.100, s32[]{:T(128)S(6)} %copy.92, s32[]{:T(128)} %constant.29.clone.1..sunk, s32[]{:T(128)} %constant.29.clone.1..sunk, s32[]{:T(128)} %constant.29.clone.1..sunk) | dynamic-update-slice | bytes 327684 | tf_op jit(solution)/shard_map/while/body/jit(dynamic_update_index_in_dim)/dynamic_update_slice | solution.py:111
  197.9 5.5 %dynamic_update_slice.14 = f32[8,128,5,64]{1,0,3,2:T(8,128)} dynamic-update-slice(f32[8,128,5,64]{1,0,3,2:T(8,128)} %get-tuple-element.298, f32[1,128,5,64]{1,0,3,2:T(1,128)S(1)} %bitcast.100, s32[]{:T(128)S(6)} %copy.92, s32[]{:T(128)} %constant.29.clone.1..sunk, s32[]{:T(128)} %constant.29.clone.1..sunk, s32[]{:T(128)} %constant.29.clone.1..sunk) | dynamic-update-slice | bytes 327684 | tf_op jit(solution)/shard_map/while/body/jit(dynamic_update_index_in_dim)/dynamic_update_slice | solution.py:111
  205.4 1.4 constant_dynamic-slice_fusion.2
  208.6 5.5 %dynamic_update_slice.14 = f32[8,128,5,64]{1,0,3,2:T(8,128)} dynamic-update-slice(f32[8,128,5,64]{1,0,3,2:T(8,128)} %get-tuple-element.298, f32[1,128,5,64]{1,0,3,2:T(1,128)S(1)} %bitcast.100, s32[]{:T(128)S(6)} %copy.92, s32[]{:T(128)} %constant.29.clone.1..sunk, s32[]{:T(128)} %constant.29.clone.1..sunk, s32[]{:T(128)} %constant.29.clone.1..sunk) | dynamic-update-slice | bytes 327684 | tf_op jit(solution)/shard_map/while/body/jit(dynamic_update_index_in_dim)/dynamic_update_slice | solution.py:111
  219.3 5.5 %dynamic_update_slice.14 = f32[8,128,5,64]{1,0,3,2:T(8,128)} dynamic-update-slice(f32[8,128,5,64]{1,0,3,2:T(8,128)} %get-tuple-element.298, f32[1,128,5,64]{1,0,3,2:T(1,128)S(1)} %bitcast.100, s32[]{:T(128)S(6)} %copy.92, s32[]{:T(128)} %constant.29.clone.1..sunk, s32[]{:T(128)} %constant.29.clone.1..sunk, s32[]{:T(128)} %constant.29.clone.1..sunk) | dynamic-update-slice | bytes 327684 | tf_op jit(solution)/shard_map/while/body/jit(dynamic_update_index_in_dim)/dynamic_update_slice | solution.py:111
  230.0 5.5 %dynamic_update_slice.14 = f32[8,128,5,64]{1,0,3,2:T(8,128)} dynamic-update-slice(f32[8,128,5,64]{1,0,3,2:T(8,128)} %get-tuple-element.298, f32[1,128,5,64]{1,0,3,2:T(1,128)S(1)} %bitcast.100, s32[]{:T(128)S(6)} %copy.92, s32[]{:T(128)} %constant.29.clone.1..sunk, s32[]{:T(128)} %constant.29.clone.1..sunk, s32[]{:T(128)} %constant.29.clone.1..sunk) | dynamic-update-slice | bytes 327684 | tf_op jit(solution)/shard_map/while/body/jit(dynamic_update_index_in_dim)/dynamic_update_slice | solution.py:111
  240.7 5.5 %dynamic_update_slice.14 = f32[8,128,5,64]{1,0,3,2:T(8,128)} dynamic-update-slice(f32[8,128,5,64]{1,0,3,2:T(8,128)} %get-tuple-element.298, f32[1,128,5,64]{1,0,3,2:T(1,128)S(1)} %bitcast.100, s32[]{:T(128)S(6)} %copy.92, s32[]{:T(128)} %constant.29.clone.1..sunk, s32[]{:T(128)} %constant.29.clone.1..sunk, s32[]{:T(128)} %constant.29.clone.1..sunk) | dynamic-update-slice | bytes 327684 | tf_op jit(solution)/shard_map/while/body/jit(dynamic_update_index_in_dim)/dynamic_update_slice | solution.py:111
  251.4 5.5 %dynamic_update_slice.14 = f32[8,128,5,64]{1,0,3,2:T(8,128)} dynamic-update-slice(f32[8,128,5,64]{1,0,3,2:T(8,128)} %get-tuple-element.298, f32[1,128,5,64]{1,0,3,2:T(1,128)S(1)} %bitcast.100, s32[]{:T(128)S(6)} %copy.92, s32[]{:T(128)} %constant.29.clone.1..sunk, s32[]{:T(128)} %constant.29.clone.1..sunk, s32[]{:T(128)} %constant.29.clone.1..sunk) | dynamic-update-slice | bytes 327684 | tf_op jit(solution)/shard_map/while/body/jit(dynamic_update_index_in_dim)/dynamic_update_slice | solution.py:111
  262.1 5.5 %dynamic_update_slice.14 = f32[8,128,5,64]{1,0,3,2:T(8,128)} dynamic-update-slice(f32[8,128,5,64]{1,0,3,2:T(8,128)} %get-tuple-element.298, f32[1,128,5,64]{1,0,3,2:T(1,128)S(1)} %bitcast.100, s32[]{:T(128)S(6)} %copy.92, s32[]{:T(128)} %constant.29.clone.1..sunk, s32[]{:T(128)} %constant.29.clone.1..sunk, s32[]{:T(128)} %constant.29.clone.1..sunk) | dynamic-update-slice | bytes 327684 | tf_op jit(solution)/shard_map/while/body/jit(dynamic_update_index_in_dim)/dynamic_update_slice | solution.py:111
  268.9 2.5 reshape.135
  271.4 87.8 %while.27 = (s32[]{:T(128)}, f32[5,64,128]{2,1,0:T(8,128)S(1)}, f32[5]{0:T(128)S(1)}, f32[5,64,128]{2,1,0:T(8,128)S(1)}, s32[]{:T(128)}) while((s32[]{:T(128)}, f32[5,64,128]{2,1,0:T(8,128)S(1)}, f32[5]{0:T(128)S(1)}, f32[5,64,128]{2,1,0:T(8,128)S(1)}, s32[]{:T(128)}) %tuple.58), condition=%wide.region_4.5_spmd, body=%wide.region_3.4_spmd.sunk | while | flops 81922 | bytes 1147001 | solution.py:119
  271.5 1.9 collective-permute-start
  273.4 10.2 %collective-permute-done = f32[5,64,128]{2,1,0:T(8,128)S(1)} collective-permute-done((f32[5,64,128]{2,1,0:T(8,128)S(1)}, f32[5,64,128]{2,1,0:T(8,128)S(1)}, u32[]{:S(2)}, u32[]{:S(2)}) %collective-permute-start) | collective-permute-done | bytes 163872 | tf_op jit(solution)/shard_map/while/body/eval_jaxpr/ppermute | solution.py:17
  283.7 1.9 collective-permute-start
  285.7 9.0 %collective-permute-done = f32[5,64,128]{2,1,0:T(8,128)S(1)} collective-permute-done((f32[5,64,128]{2,1,0:T(8,128)S(1)}, f32[5,64,128]{2,1,0:T(8,128)S(1)}, u32[]{:S(2)}, u32[]{:S(2)}) %collective-permute-start) | collective-permute-done | bytes 163872 | tf_op jit(solution)/shard_map/while/body/eval_jaxpr/ppermute | solution.py:17
  294.7 1.9 collective-permute-start
  296.6 11.2 %collective-permute-done = f32[5,64,128]{2,1,0:T(8,128)S(1)} collective-permute-done((f32[5,64,128]{2,1,0:T(8,128)S(1)}, f32[5,64,128]{2,1,0:T(8,128)S(1)}, u32[]{:S(2)}, u32[]{:S(2)}) %collective-permute-start) | collective-permute-done | bytes 163872 | tf_op jit(solution)/shard_map/while/body/eval_jaxpr/ppermute | solution.py:17
  308.0 1.9 collective-permute-start
  309.9 9.4 %collective-permute-done = f32[5,64,128]{2,1,0:T(8,128)S(1)} collective-permute-done((f32[5,64,128]{2,1,0:T(8,128)S(1)}, f32[5,64,128]{2,1,0:T(8,128)S(1)}, u32[]{:S(2)}, u32[]{:S(2)}) %collective-permute-start) | collective-permute-done | bytes 163872 | tf_op jit(solution)/shard_map/while/body/eval_jaxpr/ppermute | solution.py:17
  319.3 1.9 collective-permute-start
  321.3 11.2 %collective-permute-done = f32[5,64,128]{2,1,0:T(8,128)S(1)} collective-permute-done((f32[5,64,128]{2,1,0:T(8,128)S(1)}, f32[5,64,128]{2,1,0:T(8,128)S(1)}, u32[]{:S(2)}, u32[]{:S(2)}) %collective-permute-start) | collective-permute-done | bytes 163872 | tf_op jit(solution)/shard_map/while/body/eval_jaxpr/ppermute | solution.py:17
  332.6 1.9 collective-permute-start
  334.5 12.5 %collective-permute-done = f32[5,64,128]{2,1,0:T(8,128)S(1)} collective-permute-done((f32[5,64,128]{2,1,0:T(8,128)S(1)}, f32[5,64,128]{2,1,0:T(8,128)S(1)}, u32[]{:S(2)}, u32[]{:S(2)}) %collective-permute-start) | collective-permute-done | bytes 163872 | tf_op jit(solution)/shard_map/while/body/eval_jaxpr/ppermute | solution.py:17
  347.1 1.9 collective-permute-start
  349.0 10.2 %collective-permute-done = f32[5,64,128]{2,1,0:T(8,128)S(1)} collective-permute-done((f32[5,64,128]{2,1,0:T(8,128)S(1)}, f32[5,64,128]{2,1,0:T(8,128)S(1)}, u32[]{:S(2)}, u32[]{:S(2)}) %collective-permute-start) | collective-permute-done | bytes 163872 | tf_op jit(solution)/shard_map/while/body/eval_jaxpr/ppermute | solution.py:17
  359.2 2.1 fusion.35
  361.3 1.6 copy.63
  362.9 1.9 convert_element_type.89
  364.8 22.9 %all-to-all-start = ((bf16[32,32,320]{2,1,0:T(8,128)(2,1)}), bf16[32,32,320]{2,1,0:T(8,128)(2,1)S(1)}, u32[]{:S(2)}, u32[]{:S(2)}) async-start(bf16[32,32,320]{2,1,0:T(8,128)(2,1)} %convert_element_type.89), calls=%async_computation | async-start | bytes 1572864 | tf_op jit(solution)/shard_map/all_to_all | solution.py:135
  390.0 1.7 reshape.138
  391.8 2.3 reshape.140
  394.1 15.2 %all-to-all-done = bf16[32,32,320]{2,1,0:T(8,128)(2,1)S(1)} async-done(((bf16[32,32,320]{2,1,0:T(8,128)(2,1)}), bf16[32,32,320]{2,1,0:T(8,128)(2,1)S(1)}, u32[]{:S(2)}, u32[]{:S(2)}) %all-to-all-start) | async-done | bytes 655392 | tf_op jit(solution)/shard_map/all_to_all | solution.py:135
  410.4 1.7 reshape.137
  412.1 2.3 reshape.139
  414.4 3.0 multiply_reduce_fusion
  (205 shorter events, 57.2 us)
Async XLA Ops:
  6.5 105.8 %copy-start = (bf16[8192,64]{0,1:T(8,128)(2,1)S(1)}, bf16[8192,64]{0,1:T(8,128)(2,1)}, u32[]{:S(2)}) copy-start(bf16[8192,64]{0,1:T(8,128)(2,1)} %param.18) | copy-start | bytes 3145732
  6.5 105.8 %all-gather.2.cloned.1.call-start = ((), (), s32[]{:S(2)}) async-start(), calls=%async_computation.2 | async-start | bytes 17301504 | tf_op jit(solution)/shard_map/all_gather | solution.py:51
  112.3 18.7 %copy-start.2 = (bf16[1024,8192]{1,0:T(8,128)(2,1)S(1)}, bf16[1024,8192]{1,0:T(8,128)(2,1)}, u32[]{:S(2)}) copy-start(bf16[1024,8192]{1,0:T(8,128)(2,1)} %all-gather.2.cloned.1.call-done) | copy-start | bytes 50331652
  123.4 23.9 %slice-start = ((s8[5242880]{0:T(1024)(128)(4,1)}), s8[4194304]{0:T(1024)(128)(4,1)S(1)}, s32[]{:S(2)}) async-start(s8[5242880]{0:T(1024)(128)(4,1)} %bitcast.113), calls=%async_computation.3 | async-start | bytes 8388608
  123.5 23.8 %slice-start.1 = ((s8[5242880]{0:T(1024)(128)(4,1)}), s8[1048576]{0:T(1024)(128)(4,1)S(1)}, s32[]{:S(2)}) async-start(s8[5242880]{0:T(1024)(128)(4,1)} %bitcast.113), calls=%async_computation.4 | async-start | bytes 2097152
  123.5 29.4 %collective-permute-start.2 = (bf16[3,64]{0,1:T(8,128)(2,1)S(1)}, bf16[3,64]{0,1:T(8,128)(2,1)S(1)}, u32[]{:S(2)}, u32[]{:S(2)}) collective-permute-start(bf16[3,64]{0,1:T(8,128)(2,1)S(1)} %slice.90), channel_id=1, source_target_pairs={{0,32},{32,64},{64,96},{96,128},{128,160},{160,192},{192,224},{1,3... | collective-permute-start | bytes 1160 | tf_op jit(solution)/shard_map/ppermute | solution.py:17
  145.1 8.9 %copy-start.5 = (bf16[8192,5]{0,1:T(8,128)(2,1)S(1)}, bf16[8192,5]{0,1:T(8,128)(2,1)}, u32[]{:S(2)}) copy-start(bf16[8192,5]{0,1:T(8,128)(2,1)} %param.19) | copy-start | bytes 245764
  145.1 8.9 %copy-start.7 = (f32[5]{0:T(128)S(1)}, f32[5]{0:T(128)}, u32[]{:S(2)}) copy-start(f32[5]{0:T(128)} %param.22) | copy-start | bytes 64
  145.1 19.6 %collective-permute-start.1 = (bf16[3,320]{0,1:T(8,128)(2,1)S(1)}, bf16[3,320]{0,1:T(8,128)(2,1)S(1)}, u32[]{:S(2)}, u32[]{:S(2)}) collective-permute-start(bf16[3,320]{0,1:T(8,128)(2,1)S(1)} %slice.85), channel_id=1, source_target_pairs={{0,32},{32,64},{64,96},{96,128},{128,160},{160,192},{192,224},{1,3... | collective-permute-start | bytes 5768 | tf_op jit(solution)/shard_map/ppermute | solution.py:17
  153.3 11.4 %collective-permute-start.3 = (bf16[1024,64]{0,1:T(8,128)(2,1)S(1)}, bf16[1024,64]{0,1:T(8,128)(2,1)S(1)}, u32[]{:S(2)}, u32[]{:S(2)}) collective-permute-start(bf16[1024,64]{0,1:T(8,128)(2,1)S(1)} %multiply_convert_fusion.2), channel_id=1, source_target_pairs={{0,1},{1,0},{2,3},{3,2},{4,5},{5,4},{6,7},{7,6},{8,9},{9,8},{10,11... | collective-permute-start | bytes 393224 | tf_op jit(solution)/shard_map/ppermute | solution.py:23
  159.8 205.0 %all-to-all-start.1 = ((bf16[32,32,320]{2,1,0:T(8,128)(2,1)}), bf16[32,32,320]{2,1,0:T(8,128)(2,1)}, u32[]{:S(2)}, u32[]{:S(2)}) async-start(bf16[32,32,320]{2,1,0:T(8,128)(2,1)} %bitcast.11), calls=%async_computation.1 | async-start | bytes 1572864 | tf_op jit(solution)/shard_map/all_to_all | solution.py:136
  164.8 14.8 %collective-permute-start.4 = (bf16[1024,128]{0,1:T(8,128)(2,1)S(1)}, bf16[1024,128]{0,1:T(8,128)(2,1)}, u32[]{:S(2)}, u32[]{:S(2)}) collective-permute-start(bf16[1024,128]{0,1:T(8,128)(2,1)S(1)} %maximum_select_fusion.1), channel_id=1, source_target_pairs={{0,2},{1,3},{2,0},{3,1},{4,6},{5,7},{6,4},{7,5},{8,10},{9,11},{10,... | collective-permute-start | bytes 786440 | tf_op jit(solution)/shard_map/ppermute | solution.py:23
  271.4 87.8 %copy-start.8 = (f32[5]{0:T(128)S(1)}, f32[5]{0:T(128)}, u32[]{:S(2)}) copy-start(f32[5]{0:T(128)} %param.24) | copy-start | bytes 64
  271.5 12.1 %collective-permute-start = (f32[5,64,128]{2,1,0:T(8,128)S(1)}, f32[5,64,128]{2,1,0:T(8,128)S(1)}, u32[]{:S(2)}, u32[]{:S(2)}) collective-permute-start(f32[5,64,128]{2,1,0:T(8,128)S(1)} %multiply_add_fusion.2), channel_id=1, source_target_pairs={{0,32},{32,64},{64,96},{96,128},{128,160},{160,192},{192,224},{1,3... | collective-permute-start | bytes 491528 | tf_op jit(solution)/shard_map/while/body/eval_jaxpr/ppermute | solution.py:17
  283.7 10.9 %collective-permute-start = (f32[5,64,128]{2,1,0:T(8,128)S(1)}, f32[5,64,128]{2,1,0:T(8,128)S(1)}, u32[]{:S(2)}, u32[]{:S(2)}) collective-permute-start(f32[5,64,128]{2,1,0:T(8,128)S(1)} %multiply_add_fusion.2), channel_id=1, source_target_pairs={{0,32},{32,64},{64,96},{96,128},{128,160},{160,192},{192,224},{1,3... | collective-permute-start | bytes 491528 | tf_op jit(solution)/shard_map/while/body/eval_jaxpr/ppermute | solution.py:17
  294.7 13.2 %collective-permute-start = (f32[5,64,128]{2,1,0:T(8,128)S(1)}, f32[5,64,128]{2,1,0:T(8,128)S(1)}, u32[]{:S(2)}, u32[]{:S(2)}) collective-permute-start(f32[5,64,128]{2,1,0:T(8,128)S(1)} %multiply_add_fusion.2), channel_id=1, source_target_pairs={{0,32},{32,64},{64,96},{96,128},{128,160},{160,192},{192,224},{1,3... | collective-permute-start | bytes 491528 | tf_op jit(solution)/shard_map/while/body/eval_jaxpr/ppermute | solution.py:17
  308.0 11.3 %collective-permute-start = (f32[5,64,128]{2,1,0:T(8,128)S(1)}, f32[5,64,128]{2,1,0:T(8,128)S(1)}, u32[]{:S(2)}, u32[]{:S(2)}) collective-permute-start(f32[5,64,128]{2,1,0:T(8,128)S(1)} %multiply_add_fusion.2), channel_id=1, source_target_pairs={{0,32},{32,64},{64,96},{96,128},{128,160},{160,192},{192,224},{1,3... | collective-permute-start | bytes 491528 | tf_op jit(solution)/shard_map/while/body/eval_jaxpr/ppermute | solution.py:17
  319.3 13.1 %collective-permute-start = (f32[5,64,128]{2,1,0:T(8,128)S(1)}, f32[5,64,128]{2,1,0:T(8,128)S(1)}, u32[]{:S(2)}, u32[]{:S(2)}) collective-permute-start(f32[5,64,128]{2,1,0:T(8,128)S(1)} %multiply_add_fusion.2), channel_id=1, source_target_pairs={{0,32},{32,64},{64,96},{96,128},{128,160},{160,192},{192,224},{1,3... | collective-permute-start | bytes 491528 | tf_op jit(solution)/shard_map/while/body/eval_jaxpr/ppermute | solution.py:17
  332.6 14.4 %collective-permute-start = (f32[5,64,128]{2,1,0:T(8,128)S(1)}, f32[5,64,128]{2,1,0:T(8,128)S(1)}, u32[]{:S(2)}, u32[]{:S(2)}) collective-permute-start(f32[5,64,128]{2,1,0:T(8,128)S(1)} %multiply_add_fusion.2), channel_id=1, source_target_pairs={{0,32},{32,64},{64,96},{96,128},{128,160},{160,192},{192,224},{1,3... | collective-permute-start | bytes 491528 | tf_op jit(solution)/shard_map/while/body/eval_jaxpr/ppermute | solution.py:17
  347.1 12.1 %collective-permute-start = (f32[5,64,128]{2,1,0:T(8,128)S(1)}, f32[5,64,128]{2,1,0:T(8,128)S(1)}, u32[]{:S(2)}, u32[]{:S(2)}) collective-permute-start(f32[5,64,128]{2,1,0:T(8,128)S(1)} %multiply_add_fusion.2), channel_id=1, source_target_pairs={{0,32},{32,64},{64,96},{96,128},{128,160},{160,192},{192,224},{1,3... | collective-permute-start | bytes 491528 | tf_op jit(solution)/shard_map/while/body/eval_jaxpr/ppermute | solution.py:17
  364.8 44.5 %all-to-all-start = ((bf16[32,32,320]{2,1,0:T(8,128)(2,1)}), bf16[32,32,320]{2,1,0:T(8,128)(2,1)S(1)}, u32[]{:S(2)}, u32[]{:S(2)}) async-start(bf16[32,32,320]{2,1,0:T(8,128)(2,1)} %convert_element_type.89), calls=%async_computation | async-start | bytes 1572864 | tf_op jit(solution)/shard_map/all_to_all | solution.py:135
  417.7 1.3 copy-start.3
  417.7 1.7 copy-start.4
  417.7 1.7 copy-start.6
  418.5 2.2 copy-start.1
Sparse Core Ops, SparseCore 0:
  9.2 103.0 all-gather.1
where the time goes:
time: 429 us; the launch traced here: 427 us
  waiting for transfers between devices  199 us (46%)
  local copies, waits for them, and re-layouts  90.2 us (21%)
  starting transfers between devices  53.1 us (12%)
  matrix products  51 us (12%)
  other arithmetic  19.8 us (5%)
  between operations  13.8 us (3%)
    all_gather x1, waiting for transfers between devices, shards(): piece = lax.all_gather(tokens, 'head', axis=0, tiled=True)  103 us
    ppermute x9, waiting for transfers between devices, passed_along(): lax.ppermute(value, axis, [(source, source + steps) for source in range(l...  73.6 us
    dynamic_update_slice x8, local copies, waits for them, and re-layouts, shards(): lax.scan(advance, start, (xs, bcs, decays, steps_all))  43.6 us
    ppermute x9, starting transfers between devices, passed_along(): lax.ppermute(value, axis, [(source, source + steps) for source in range(l...  23.1 us
    all_to_all x1, starting transfers between devices, shards(): lax.all_to_all(y_ssd, 'head', split_axis=0, concat_axis=1, tiled=True)  22.9 us
    all_to_all x1, waiting for transfers between devices, shards(): lax.all_to_all(y_ssd, 'head', split_axis=0, concat_axis=1, tiled=True)  15.2 us
    dot_general x1, matrix products, shards(): jnp.dot(piece, in_x_weight, preferred_element_type=jnp.float32)  14 us
    dynamic_slice x8, local copies, waits for them, and re-layouts, shards(): lax.scan(advance, start, (xs, bcs, decays, steps_all))  11.5 us
  transfers between devices with their start and end apart: 14, of which 10 were waited for; matrix products, arithmetic and copies ran while one was open for 32% of the time, Pallas kernels for 0%

commit v1 on v0

v1 whole, which is shorter than its diff:
```python
import jax
import jax.numpy as jnp
from jax import lax
from jax.experimental import pallas as pl
from jax.experimental.pallas import tpu as pltpu
from jax.sharding import PartitionSpec as P

MESH = pl.DeviceIdType.MESH
KC = 2048


def remote(src, dst, send, recv, head):
    return pltpu.make_async_remote_copy(
        src_ref=src, dst_ref=dst, send_sem=send, recv_sem=recv,
        device_id={"head": head}, device_id_type=MESH,
    )


def gather_kernel(tok, wx, wz, wbc, wdt, pre, dt,
                  buf, wt, res, zs, zr, ys, yr, ds, dr, lsem):
    h = lax.axis_index("head")
    z, y, c = h // 8, (h // 2) % 4, h % 2
    at = lambda zz, yy: zz * 8 + yy * 2 + c
    right, left, far = (y + 1) % 4, (y + 3) % 4, (y + 2) % 4
    sib = z * 8 + y * 2 + (1 - c)
    zz = jnp.where(z < 2, z, 3 - z)
    order = [jnp.where(z < 2, q, 3 - q) for q in (zz, 1 - zz, 2, 3)]
    width = wx.shape[0]
    nbc = wbc.shape[0]

    own = pltpu.make_async_copy(tok, buf.at[h], lsem.at[0])
    own.start()
    barrier = pltpu.get_barrier_semaphore()
    for peer in (at(z, right), at(z, left), sib):
        pl.semaphore_signal(barrier, inc=1, device_id={"head": peer}, device_id_type=MESH)

    @pl.when(z > 0)
    def _():
        pl.semaphore_signal(barrier, inc=1, device_id={"head": at(z - 1, y)}, device_id_type=MESH)

    @pl.when(z < 3)
    def _():
        pl.semaphore_signal(barrier, inc=1, device_id={"head": at(z + 1, y)}, device_id_type=MESH)

    pl.semaphore_wait(barrier, 3 + (z > 0).astype(jnp.int32) + (z < 3).astype(jnp.int32))
    own.wait()

    def zcopy(p, sign):
        slot = buf.at[at(p, y)]
        return remote(slot, slot, zs.at[p, (sign + 1) // 2], zr.at[p], at(z + sign, y))

    def zsend(p, sign, act):
        toward = (p <= z) if sign > 0 else (p >= z)
        room = (z < 3) if sign > 0 else (z > 0)

        @pl.when(jnp.logical_and(toward, room))
        def _():
            act(zcopy(p, sign))

    def ycopy(p, kind):
        if kind == 0:
            return remote(buf.at[at(p, y)], buf.at[at(p, y)], ys.at[p, 0], yr.at[p, 0], at(z, right))
        if kind == 1:
            return remote(buf.at[at(p, y)], buf.at[at(p, y)], ys.at[p, 1], yr.at[p, 1], at(z, left))
        if kind == 2:
            part = buf.at[at(p, left), pl.ds(0, 16)]
            return remote(part, part, ys.at[p, 2], yr.at[p, 2], at(z, right))
        part = buf.at[at(p, right), pl.ds(16, 16)]
        return remote(part, part, ys.at[p, 3], yr.at[p, 3], at(z, left))

    def ywait(p, kind):
        if kind == 0:
            part = buf.at[at(p, left)]
        elif kind == 1:
            part = buf.at[at(p, right)]
        elif kind == 2:
            part = buf.at[at(p, far), pl.ds(0, 16)]
        else:
            part = buf.at[at(p, far), pl.ds(16, 16)]
        remote(part, part, ys.at[p, kind], yr.at[p, kind], h).wait_recv()

    def dcopy(p, yy):
        slot = buf.at[at(p, yy)]
        return remote(slot, slot, ds.at[p, yy], dr.at[p, yy], sib)

    def dwait(p, yy):
        slot = buf.at[p * 8 + yy * 2 + 1 - c]
        remote(slot, slot, ds.at[p, yy], dr.at[p, yy], sib).wait_recv()

    def begin(p):
        ycopy(p, 0).start()
        ycopy(p, 1).start()
        dcopy(p, y).start()

    def near(p):
        ywait(p, 0)
        ycopy(p, 2).start()
        ywait(p, 1)
        ycopy(p, 3).start()
        dcopy(p, left).start()
        dcopy(p, right).start()

    def last(p):
        ywait(p, 2)
        ywait(p, 3)
        dcopy(p, far).start()

    def product(p):
        for yy in (y, left, right, far):
            dwait(p, yy)

        def chunk(k, _):
            ks = pl.ds(pl.multiple_of(k * KC, KC), KC)
            a = buf[pl.ds(p * 8, 8), :, ks].reshape(256, KC)
            part = lax.dot_general(wt[:, ks], a, (((1,), (1,)), ((), ())),
                                   preferred_element_type=jnp.float32)

            @pl.when(k == 0)
            def _():
                res[...] = part

            @pl.when(k > 0)
            def _():
                res[...] += part

            return 0

        lax.fori_loop(0, buf.shape[2] // KC, chunk, 0)
        span = pl.ds(pl.multiple_of(p * 256, 256), 256)
        n = pre.shape[0]
        pre[:, span] = res[0:n, :].astype(jnp.bfloat16)
        dt[:, span] = res[n : n + 16, :]

    zsend(order[0], 1, lambda d: d.start())
    zsend(order[0], -1, lambda d: d.start())
    begin(order[0])
    loads = [
        pltpu.make_async_copy(wx, wt.at[pl.ds(0, width)], lsem.at[1]),
        pltpu.make_async_copy(wz, wt.at[pl.ds(width, width)], lsem.at[2]),
        pltpu.make_async_copy(wbc, wt.at[pl.ds(2 * width, nbc)], lsem.at[3]),
    ]
    for load in loads:
        load.start()
    n = 2 * width + nbc
    wt[n : n + 16, :] = jnp.concatenate(
        [wdt[...].astype(jnp.float32), jnp.zeros((16 - wdt.shape[0], wt.shape[1]), jnp.float32)], axis=0
    ).astype(jnp.bfloat16)
    for load in loads:
        load.wait()

    for j in range(1, 4):
        p = order[j]
        slot = buf.at[at(p, y)]
        remote(slot, slot, zs.at[p, 0], zr.at[p], h).wait_recv()
        zsend(p, 1, lambda d: d.start())
        zsend(p, -1, lambda d: d.start())
        begin(p)
        near(order[j - 1])
        if j >= 2:
            last(order[j - 2])
        if j >= 3:
            product(order[j - 3])
    near(order[3])
    last(order[2])
    product(order[1])
    product(order[2])
    last(order[3])
    product(order[3])
    for j in range(4):
        p = order[j]
        zsend(p, 1, lambda d: d.wait_send())
        zsend(p, -1, lambda d: d.wait_send())
        for kind in range(4):
            ycopy(p, kind).wait_send()
        for yy in range(4):
            dcopy(p, yy).wait_send()


def gather_call(tok, wx, wz, wbc, wdt):
    d = tok.shape[1]
    n = 2 * wx.shape[0] + wbc.shape[0]
    anyspec = pl.BlockSpec(memory_space=pl.ANY)
    vm = pl.BlockSpec(memory_space=pltpu.VMEM)
    dma = pltpu.SemaphoreType.DMA
    return pl.pallas_call(
        gather_kernel,
        out_shape=(jax.ShapeDtypeStruct((n, 1024), jnp.bfloat16),
                   jax.ShapeDtypeStruct((16, 1024), jnp.float32)),
        in_specs=[anyspec] * 4 + [vm],
        out_specs=(vm, vm),
        scratch_shapes=[
            pltpu.VMEM((32, 32, d), jnp.bfloat16),
            pltpu.VMEM((n + 16, d), jnp.bfloat16),
            pltpu.VMEM((n + 16, 256), jnp.float32),
            dma((4, 2)), dma((4,)), dma((4, 4)), dma((4, 4)), dma((4, 4)), dma((4, 4)), dma((4,)),
        ],
        compiler_params=pltpu.CompilerParams(collective_id=0, has_side_effects=True,
                                             vmem_limit_bytes=60 * 2**20),
        name="gather_project",
    )(tok, wx, wz, wbc, wdt)


F32 = jnp.float32
BF16 = jnp.bfloat16
NT = (((1,), (1,)), ((), ()))
TN = (((0,), (0,)), ((), ()))


def rcopy(src, dst, send, recv, **device):
    return pltpu.make_async_remote_copy(
        src_ref=src, dst_ref=dst, send_sem=send, recv_sem=recv,
        device_id=device, device_id_type=MESH,
    )


def silu(v):
    return v / (1.0 + jnp.exp(-v))


def mix_kernel(pre, dt, cx, cbc, bias, alog, skip, gain, out,
               halo_out, halo_in, hpad, xc, bcf, step, cums, cumt, yin, sstart, sfin, tfin,
               st_in, tot_in, inc, sb, rbuf, asm,
               hs, hr, bs, br, ss, sr, ts, tr, as_, ar):
    h = lax.axis_index("head")
    s = lax.axis_index("seq")
    heads, W = 5, 320
    ZB, BB = W, 2 * W
    nseq = 8

    barrier = pltpu.get_barrier_semaphore()

    def greet(k, _):
        pl.semaphore_signal(barrier, inc=1, device_id={"head": (h + k) % 32}, device_id_type=MESH)
        return 0

    lax.fori_loop(1, 32, greet, 0)

    def greet_seq(k, _):
        pl.semaphore_signal(barrier, inc=1, device_id={"seq": (s + k) % nseq}, device_id_type=MESH)
        return 0

    lax.fori_loop(1, nseq, greet_seq, 0)
    pl.semaphore_wait(barrier, 31 + nseq - 1)

    pick = (lax.broadcasted_iota(jnp.int32, (16, 128), 1)
            == lax.broadcasted_iota(jnp.int32, (16, 128), 0) + 112).astype(BF16)
    halo_out[:, 0:W] = lax.dot_general(pick, pre[0:W, 896:1024], NT, preferred_element_type=F32).astype(BF16)
    halo_out[:, 384:448] = lax.dot_general(pick, pre[BB:BB + 64, 896:1024], NT, preferred_element_type=F32).astype(BF16)

    @pl.when(s < nseq - 1)
    def _():
        rcopy(halo_out, halo_in, hs, hr, seq=s + 1).start()

    row = lax.broadcasted_iota(jnp.int32, (8, 128), 0)
    bias_col = jnp.zeros((8, 128), F32)
    rate_col = jnp.zeros((8, 128), F32)
    for k in range(heads):
        bias_col = jnp.where(row == k, bias[k], bias_col)
        rate_col = jnp.where(row == k, alog[k], rate_col)
    rate_col = jnp.exp(rate_col)
    upper = (lax.broadcasted_iota(jnp.int32, (128, 128), 0)
             <= lax.broadcasted_iota(jnp.int32, (128, 128), 1))
    parts = []
    for b in range(8):
        v = dt[0:8, b * 128:(b + 1) * 128] + bias_col
        v = jnp.maximum(v, 0.0) + jnp.log1p(jnp.exp(-jnp.abs(v)))
        step[b * 8:(b + 1) * 8, :] = v
        parts.append(-v * rate_col)
    dec = jnp.concatenate(parts, axis=0)
    cum = jnp.dot(dec, upper.astype(F32), preferred_element_type=F32, precision=lax.Precision.HIGHEST)
    cums[...] = cum
    tot = jnp.broadcast_to(cum[:, 127:128], (64, 128))
    weight = step[...] * jnp.exp(tot - cum)
    cumt[...] = (cum - jnp.log(step[...])).T

    @pl.when(s == 0)
    def _():
        hpad[...] = jnp.zeros_like(hpad)

    @pl.when(s > 0)
    def _():
        rcopy(halo_out, halo_in, hs, hr, seq=s).wait_recv()
        hpad[0:W, :] = lax.dot_general(halo_in[:, 0:W], pick, TN, preferred_element_type=F32)
        hpad[W:W + 64, :] = lax.dot_general(halo_in[:, 384:448], pick, TN, preferred_element_type=F32)

    lane = lax.broadcasted_iota(jnp.int32, (64, 128), 1)
    tapx = jnp.concatenate([cx[...], jnp.zeros((4, W), F32)], axis=0).T
    tapb = jnp.concatenate([cbc[...], jnp.zeros((4, 64), F32)], axis=0).T

    def conv(r0, taps, hrow, dst, drow):
        prev = hpad[hrow:hrow + 64, :]
        for b in range(8):
            cur = pre[r0:r0 + 64, b * 128:(b + 1) * 128].astype(F32)
            total = taps[:, 3:4] * cur
            for k in range(1, 4):
                moved = pltpu.roll(jnp.where(lane >= 128 - k, prev, cur), k, 1)
                total = total + taps[:, 3 - k:4 - k] * moved
            dst[pl.ds(drow, 64), b * 128:(b + 1) * 128] = silu(total).astype(BF16)
            prev = cur

    mine = pl.multiple_of((h % 4) * 64, 64)
    conv(BB, tapb, W, bcf, mine)
    base = (h // 4) * 4
    slot = bcf.at[pl.ds(mine, 64)]
    for k in range(1, 4):
        rcopy(slot, slot, bs.at[k], br.at[h % 4], head=base + (h + k) % 4).start()
    for k in range(heads):
        conv(k * 64, tapx[k * 64:(k + 1) * 64], k * 64, xc, k * 64)
    for k in range(1, 4):
        q = (h + k) % 4
        other = bcf.at[pl.ds(pl.multiple_of(q * 64, 64), 64)]
        rcopy(other, other, bs.at[k], br.at[q], head=h).wait_recv()

    def rows(v, r):
        return jnp.concatenate(
            [jnp.broadcast_to(v[r + k:r + k + 1, :], (64, 128)) for k in range(heads)], axis=0)

    state = jnp.zeros((W, 128), F32)
    total = jnp.zeros((8, 128), F32)
    for b in range(8):
        cols = slice(b * 128, (b + 1) * 128)
        sstart[b] = state
        xw = (xc[:, cols].astype(F32) * rows(weight, b * 8)).astype(BF16)
        fresh = lax.dot_general(xw, bcf[0:128, cols], NT, preferred_element_type=F32)
        tb = tot[b * 8:(b + 1) * 8, :]
        state = state * rows(jnp.exp(tb), 0) + fresh
        total = total + tb
    sfin[...] = state.astype(BF16)
    tfin[...] = total
    for t in range(1, nseq):
        @pl.when(s + t < nseq)
        def _():
            rcopy(sfin, st_in.at[s], ss.at[t], sr.at[s], seq=s + t).start()
            rcopy(tfin, tot_in.at[s], ts.at[t], tr.at[s], seq=s + t).start()

    for b in range(8):
        cols = slice(b * 128, (b + 1) * 128)
        scores = lax.dot_general(bcf[0:128, cols], bcf[128:256, cols], TN, preferred_element_type=F32)
        scores = jnp.where(upper, scores, 0.0)
        for k in range(heads):
            r = b * 8 + k
            diff = cums[r:r + 1, :] - cumt[:, r:r + 1]
            mixing = jnp.exp(jnp.where(upper, diff, -jnp.inf)) * scores
            yin[k * 64:(k + 1) * 64, cols] = jnp.dot(
                xc[k * 64:(k + 1) * 64, cols], mixing.astype(BF16), preferred_element_type=F32)

    inc[...] = jnp.zeros_like(inc)
    for q in range(nseq - 1):
        @pl.when(q < s)
        def _():
            rcopy(sfin, st_in.at[q], ss.at[0], sr.at[q], seq=s).wait_recv()
            rcopy(tfin, tot_in.at[q], ts.at[0], tr.at[q], seq=s).wait_recv()
            inc[...] = inc[...] * rows(jnp.exp(tot_in[q]), 0) + st_in[q].astype(F32)

    skips = jnp.concatenate([jnp.full((64, 128), skip[k], F32) for k in range(heads)], axis=0)
    offset = jnp.zeros((8, 128), F32)
    for b in range(8):
        cols = slice(b * 128, (b + 1) * 128)
        st = (sstart[b] + inc[...] * rows(jnp.exp(offset), 0)).astype(BF16)
        yst = jnp.dot(st, bcf[128:256, cols], preferred_element_type=F32)
        y = yin[:, cols] + yst * rows(jnp.exp(cums[b * 8:(b + 1) * 8, :]), 0) + skips * xc[:, cols].astype(F32)
        y = y.astype(BF16).astype(F32)
        g = y * silu(pre[ZB:ZB + W, cols].astype(F32))
        gt = g.T
        for i in range(4):
            sb[4 * b + i, :, 0:W] = gt[32 * i:32 * i + 16, :].astype(BF16)
            sb[4 * b + i, :, W:2 * W] = gt[32 * i + 16:32 * i + 32, :].astype(BF16)
        offset = offset + tot[b * 8:(b + 1) * 8, :]

    def scatter(k, _):
        dst = (h + k) % 32
        rcopy(sb.at[dst], rbuf.at[h], as_.at[dst], ar.at[h], head=dst).start()
        return 0

    lax.fori_loop(1, 32, scatter, 0)
    rbuf[h] = sb[h]

    def collect(k, _):
        src = (h + k) % 32
        rcopy(sb.at[src], rbuf.at[src], as_.at[src], ar.at[src], head=h).wait_recv()
        return 0

    lax.fori_loop(1, 32, collect, 0)

    for q in range(32):
        asm[0:16, q * W:(q + 1) * W] = rbuf[q, :, 0:W]
        asm[16:32, q * W:(q + 1) * W] = rbuf[q, :, W:2 * W]
    for g in range(5):
        v = asm[:, g * 2048:(g + 1) * 2048].astype(F32)
        scale = lax.rsqrt(jnp.mean(v * v, axis=1, keepdims=True) + 1e-5)
        for k in range(16):
            c0 = g * 16 + k
            out[:, c0 * 128:(c0 + 1) * 128] = (
                v[:, k * 128:(k + 1) * 128] * scale * gain[c0:c0 + 1, :]).astype(BF16)

    @pl.when(s < nseq - 1)
    def _():
        rcopy(halo_out, halo_in, hs, hr, seq=s + 1).wait_send()

    for k in range(1, 4):
        rcopy(slot, slot, bs.at[k], br.at[h % 4], head=h).wait_send()
    for t in range(1, nseq):
        @pl.when(s + t < nseq)
        def _():
            rcopy(sfin, st_in.at[s], ss.at[t], sr.at[s], seq=s).wait_send()
            rcopy(tfin, tot_in.at[s], ts.at[t], tr.at[s], seq=s).wait_send()

    def sent(k, _):
        dst = (h + k) % 32
        rcopy(sb.at[dst], rbuf.at[h], as_.at[dst], ar.at[h], head=h).wait_send()
        return 0

    lax.fori_loop(1, 32, sent, 0)


def mix_scratch():
    dma = pltpu.SemaphoreType.DMA
    vm = pltpu.VMEM
    return [
        vm((16, 512), BF16), vm((16, 512), BF16), vm((384, 128), F32),
        vm((320, 1024), BF16), vm((256, 1024), BF16), vm((64, 128), F32), vm((64, 128), F32),
        vm((128, 64), F32), vm((320, 1024), F32), vm((8, 320, 128), F32),
        vm((320, 128), BF16), vm((8, 128), F32),
        vm((8, 320, 128), BF16), vm((8, 8, 128), F32), vm((320, 128), F32),
        vm((32, 16, 640), BF16), vm((32, 16, 640), BF16), vm((32, 10240), BF16),
        dma, dma, dma((4,)), dma((4,)), dma((8,)), dma((8,)), dma((8,)), dma((8,)),
        dma((32,)), dma((32,)),
    ]


def mix_call(pre, dt, cx, cbc, bias, alog, skip, gain):
    vm = pl.BlockSpec(memory_space=pltpu.VMEM)
    sm = pl.BlockSpec(memory_space=pltpu.SMEM)
    return pl.pallas_call(
        mix_kernel,
        out_shape=jax.ShapeDtypeStruct((32, 10240), BF16),
        in_specs=[vm] * 4 + [sm] * 3 + [vm],
        out_specs=vm,
        scratch_shapes=mix_scratch(),
        compiler_params=pltpu.CompilerParams(collective_id=1, has_side_effects=True,
                                             vmem_limit_bytes=60 * 2**20),
        name="mix",
    )(pre, dt, cx, cbc, bias, alog, skip, gain.reshape(80, 128))


def shards(tokens, wx, wz, wbc, wdt, cx, cbc, bias, alog, skip, gain):
    pre, dt = gather_call(tokens, wx.T, wz.T, wbc.T, wdt.T)
    return mix_call(pre, dt, cx, cbc, bias, alog, skip, gain)


def solution(mesh):
    cols = P(None, "head")
    placed = (P(("seq", "head"), None), cols, cols, cols, cols, cols, cols,
              P("head"), P("head"), P("head"), P())
    return jax.shard_map(
        shards, mesh=mesh, in_specs=placed, out_specs=P(("seq", "head"), None), check_vma=False
    )
```

time: 429 us -> 143 us (0.33)
  the two profiles are of different devices: /device:TPU:7 before, /device:TPU:255 now
where the time goes in v1:
time: 143 us
  Pallas kernels  141 us (99%)
  local copies, waits for them, and re-layouts  1.97 us (1%)
    pallas_call x1, Pallas kernels, gather_call(): pl.pallas_call(gather_kernel, out_shape=(jax.ShapeDtypeStruct((n, 1024),...  85.4 us
    pallas_call x1, Pallas kernels, mix_call(): pl.pallas_call(mix_kernel, out_shape=jax.ShapeDtypeStruct((32, 10240), BF...  55.6 us

profile of v1, /device:TPU:255, one launch (start us, length us, event | category | flops | bytes accessed | tf_op | source)
XLA Modules:
  0.0 143.0 jit_solution(12049080485551975529)
XLA Ops:
  0.0 85.4 %gather_project.1 = (bf16[704,1024]{1,0:T(8,128)(2,1)}, f32[16,1024]{1,0:T(8,128)}) custom-call(bf16[32,8192]{1,0:T(8,128)(2,1)} %tok.1, bf16[320,8192]{1,0:T(8,128)(2,1)} %bitcast.5, bf16[320,8192]{1,0:T(8,128)(2,1)} %bitcast.6, bf16[64,8192]{1,0:T(8,128)(2,1)} %bitcast.7, bf16[5,8192]{1,0:T(8,128)(2,1)} %bitcast.8), custom_call_target="tpu_custom_call" | custom-call | tf_op jit(solution)/shard_map/gather_project/pallas_call | solution.py:185
  85.4 55.6 %mix.1 = bf16[32,10240]{1,0:T(8,128)(2,1)} custom-call(bf16[704,1024]{1,0:T(8,128)(2,1)} %get-tuple-element.7.pre, f32[16,1024]{1,0:T(8,128)} %get-tuple-element.8.dt, f32[4,320]{1,0:T(4,128)} %cx.1, f32[4,64]{1,0:T(4,128)} %cbc.1, f32[5]{0:T(128)} %bias.1, f32[5]{0:T(128)} %alog.1, f32[5]{0:T(128)} %skip.1, f32[80,128]{1,0:T(8,128)} %bitcast.9), custom_call_target="tpu_custom_call" | custom-call | tf_op jit(solution)/shard_map/mix/pallas_call | solution.py:434
  141.0 2.0 %copy.13 = bf16[32,10240]{1,0:T(8,128)(2,1)} copy(bf16[32,10240]{1,0:T(8,128)(2,1)} %mix.1) | data formatting | bytes 1310720

commit v2 on v1

v2 whole, which is shorter than its diff:
```python
import jax
import jax.numpy as jnp
from jax import lax
from jax.experimental import pallas as pl
from jax.experimental.pallas import tpu as pltpu
from jax.sharding import PartitionSpec as P

MESH = pl.DeviceIdType.MESH
F32 = jnp.float32
BF16 = jnp.bfloat16
NT = (((1,), (1,)), ((), ()))
TN = (((0,), (0,)), ((), ()))
KC = 4096
EARLY = 1536
HEADS = 5
W = 320
BB = 2 * W
FIRST = W + 80
NSEQ = 8


def rcopy(src, dst, send, recv, **device):
    return pltpu.make_async_remote_copy(
        src_ref=src, dst_ref=dst, send_sem=send, recv_sem=recv,
        device_id=device, device_id_type=MESH,
    )


def silu(v):
    return v / (1.0 + jnp.exp(-v))


def kernel(tok, wx, wz, wbc, wdt, cx, cbc, bias, alog, skip, gain, out,
           buf, wt, res, pre, dt, bcp, bcf, halo_x, halo_b, in_x, in_b, hpad, taps, xc,
           step, cums, cumt, yin, sstart, sfin, tfin, st_in, tot_in, inc, sb, rbuf, asm,
           lsem, zs, zr, es, er, ys, yr, ds, dr, fs, fr,
           bs, br, cs, cr, hxs, hxr, hbs, hbr, ss, sr, ts, tr, as_, ar):
    h = lax.axis_index("head")
    s = lax.axis_index("seq")
    z, y, c = h // 8, (h // 2) % 4, h % 2
    right, left, far = (y + 1) % 4, (y + 3) % 4, (y + 2) % 4
    sib = h + 1 - 2 * c
    across = h + 2 - 4 * (y % 2)
    base = (h // 4) * 4
    quarter = h % 4
    zz = jnp.where(z < 2, z, 3 - z)
    order = [jnp.where(z < 2, q, 3 - q) for q in (zz, 1 - zz, 2, 3)]

    def at(p, yy):
        return p * 8 + yy * 2 + c

    own = pltpu.make_async_copy(tok, buf.at[h], lsem.at[0])
    own.start()
    loads = [
        pltpu.make_async_copy(wx, wt.at[pl.ds(0, W)], lsem.at[1]),
        pltpu.make_async_copy(wz, wt.at[pl.ds(FIRST, W)], lsem.at[2]),
        pltpu.make_async_copy(wbc, wt.at[pl.ds(W, 64)], lsem.at[3]),
    ]
    barrier = pltpu.get_barrier_semaphore()

    def greet(k, _):
        pl.semaphore_signal(barrier, inc=1, device_id={"head": (h + k) % 32}, device_id_type=MESH)
        return 0

    def greet_seq(k, _):
        pl.semaphore_signal(barrier, inc=1, device_id={"seq": (s + k) % NSEQ}, device_id_type=MESH)
        return 0

    lax.fori_loop(1, 32, greet, 0)
    lax.fori_loop(1, NSEQ, greet_seq, 0)

    @pl.when(s > 0)
    def _():
        for k in range(1, 4):
            pl.semaphore_signal(barrier, inc=1, device_id={"seq": s - 1, "head": base + (h + k) % 4},
                                device_id_type=MESH)

    pl.semaphore_wait(barrier, 31 + NSEQ - 1 + 3 * (s < NSEQ - 1).astype(jnp.int32))
    own.wait()

    early = pl.ds(0, EARLY)
    late = pl.ds(EARLY, buf.shape[2] - EARLY)

    def along(p, sign, act):
        toward = (p <= z) if sign > 0 else (p >= z)
        room = (z < 3) if sign > 0 else (z > 0)

        @pl.when(jnp.logical_and(toward, room))
        def _():
            slot = buf.at[at(p, y)]
            act(rcopy(slot, slot, zs.at[p, (sign + 1) // 2], zr.at[p], head=at(z + sign, y)))

    def along_early(p, yy, sign, act):
        toward = (p <= z) if sign > 0 else (p >= z)
        room = (z < 3) if sign > 0 else (z > 0)

        @pl.when(jnp.logical_and(toward, room))
        def _():
            slot = buf.at[at(p, yy), :, early]
            act(rcopy(slot, slot, es.at[p, yy, (sign + 1) // 2], er.at[p, yy], head=at(z + sign, y)))

    def both(move, *where):
        move(*where, 1, lambda d: d.start())
        move(*where, -1, lambda d: d.start())

    def ring(p, kind, own_plane):
        cols = pl.ds(0, buf.shape[2]) if own_plane else late
        yy, rows, to = (
            (y, pl.ds(0, 32), right), (y, pl.ds(0, 32), left),
            (left, pl.ds(0, 16), right), (right, pl.ds(16, 16), left),
        )[kind]
        part = buf.at[at(p, yy), rows, cols]
        return rcopy(part, part, ys.at[p, kind], yr.at[p, kind], head=at(z, to))

    def ring_wait(p, kind, own_plane):
        cols = pl.ds(0, buf.shape[2]) if own_plane else late
        yy, rows = ((left, pl.ds(0, 32)), (right, pl.ds(0, 32)),
                    (far, pl.ds(0, 16)), (far, pl.ds(16, 16)))[kind]
        part = buf.at[at(p, yy), rows, cols]
        rcopy(part, part, ys.at[p, kind], yr.at[p, kind], head=h).wait_recv()

    def twin(p, yy, whole):
        slot = buf.at[at(p, yy)] if whole else buf.at[at(p, yy), :, late]
        return rcopy(slot, slot, ds.at[p, yy], dr.at[p, yy], head=sib)

    def twin_wait(p, yy, whole):
        slot = buf.at[p * 8 + yy * 2 + 1 - c]
        slot = slot if whole else slot.at[:, late]
        rcopy(slot, slot, ds.at[p, yy], dr.at[p, yy], head=h).wait_recv()

    def twin_early(p, yy):
        slot = buf.at[at(p, yy), :, early]
        return rcopy(slot, slot, fs.at[p, yy], fr.at[p, yy], head=sib)

    def twin_early_wait(p, yy):
        slot = buf.at[p * 8 + yy * 2 + 1 - c, :, early]
        rcopy(slot, slot, fs.at[p, yy], fr.at[p, yy], head=h).wait_recv()

    def begin(p, own_plane):
        ring(p, 0, own_plane).start()
        ring(p, 1, own_plane).start()
        twin(p, y, True).start()

    def arrive(p):
        slot = buf.at[at(p, y)]
        rcopy(slot, slot, zs.at[p, 0], zr.at[p], head=h).wait_recv()
        both(along, p)
        begin(p, False)

    def arrive_early(p):
        for yy in (left, right, far):
            slot = buf.at[at(p, yy), :, early]
            rcopy(slot, slot, es.at[p, yy, 0], er.at[p, yy], head=h).wait_recv()
            both(along_early, p, yy)
            twin_early(p, yy).start()

    def near(p, own_plane):
        ring_wait(p, 0, own_plane)
        ring(p, 2, own_plane).start()
        ring_wait(p, 1, own_plane)
        ring(p, 3, own_plane).start()
        for yy in (left, right):
            twin(p, yy, own_plane).start()
            if own_plane:
                both(along_early, p, yy)

    def last(p, own_plane):
        ring_wait(p, 2, own_plane)
        ring_wait(p, 3, own_plane)
        twin(p, far, own_plane).start()
        if own_plane:
            both(along_early, p, far)

    def complete(p, own_plane):
        twin_wait(p, y, True)
        for yy in (left, right, far):
            twin_wait(p, yy, own_plane)
            if not own_plane:
                twin_early_wait(p, yy)

    def product(p, r0, n):
        def chunk(k, _):
            ks = pl.ds(pl.multiple_of(k * KC, KC), KC)
            a = buf[pl.ds(p * 8, 8), :, ks].reshape(256, KC)
            part = lax.dot_general(wt[r0:r0 + n, ks], a, NT, preferred_element_type=F32)

            @pl.when(k == 0)
            def _():
                res[r0:r0 + n] = part

            @pl.when(k > 0)
            def _():
                res[r0:r0 + n] += part

            return 0

        lax.fori_loop(0, buf.shape[2] // KC, chunk, 0)

    def span_of(p):
        return pl.ds(pl.multiple_of(p * 256, 256), 256)

    def quarter_rows(q):
        return pl.ds(pl.multiple_of(q * 64, 64), 64)

    q_sib = quarter + 1 - 2 * c
    q_across = quarter + 2 - 4 * (y % 2)
    q_other = q_across + 1 - 2 * c

    def share_copy(p, kind):
        q = (quarter, quarter, q_across)[kind]
        part = bcp.at[quarter_rows(q), span_of(p)]
        return rcopy(part, part, bs.at[p, kind], br.at[p, kind], head=(sib, across, sib)[kind])

    def share_wait(p, kind):
        q = (q_sib, q_across, q_other)[kind]
        part = bcp.at[quarter_rows(q), span_of(p)]
        rcopy(part, part, bs.at[p, kind], br.at[p, kind], head=h).wait_recv()

    def store_bc(p):
        span = span_of(p)
        bcp[quarter_rows(quarter), span] = res[W:W + 64].astype(BF16)
        dt[:, span] = res[W + 64:FIRST]
        share_copy(p, 0).start()
        share_copy(p, 1).start()

    def pass_bc(p):
        share_wait(p, 1)
        share_copy(p, 2).start()

    def store_x(p):
        pre[0:W, span_of(p)] = res[0:W].astype(BF16)

    def store_z(p):
        pre[W:BB, span_of(p)] = res[FIRST:FIRST + W].astype(BF16)

    pick = (lax.broadcasted_iota(jnp.int32, (16, 128), 1)
            == lax.broadcasted_iota(jnp.int32, (16, 128), 0) + 112).astype(BF16)

    def halo_copies():
        yield rcopy(halo_x, in_x, hxs, hxr, seq=s + 1)
        for k in range(4):
            yield rcopy(halo_b, in_b.at[quarter], hbs.at[k], hbr.at[quarter], seq=s + 1, head=base + k)

    def send_halo(p):
        @pl.when(jnp.logical_and(p == 3, s < NSEQ - 1))
        def _():
            tail = pl.ds(896, 128)
            halo_x[:, 0:W] = lax.dot_general(pick, pre[0:W, tail], NT, preferred_element_type=F32).astype(BF16)
            halo_b[:, 0:64] = lax.dot_general(
                pick, bcp[quarter_rows(quarter), tail], NT, preferred_element_type=F32).astype(BF16)
            for copy in halo_copies():
                copy.start()

    def project(p, own_plane):
        complete(p, own_plane)
        product(p, 0, FIRST)
        store_bc(p)
        store_x(p)
        send_halo(p)

    def gates(p):
        product(p, FIRST, W)
        store_z(p)

    def taps_copy(k):
        slot = taps.at[quarter]
        return rcopy(slot, slot, cs.at[k], cr.at[quarter], head=base + (h + k + 1) % 4)

    def taps_wait(k):
        q = (h + k + 1) % 4
        rcopy(taps.at[q], taps.at[q], cs.at[k], cr.at[q], head=h).wait_recv()

    both(along, order[0])
    begin(order[0], True)
    for load in loads:
        load.start()
    taps[quarter, 0:4, 0:64] = cbc[...]
    for k in range(3):
        taps_copy(k).start()
    wt[W + 64:FIRST, :] = jnp.concatenate(
        [wdt[...].astype(F32), jnp.zeros((16 - HEADS, wt.shape[1]), F32)], axis=0).astype(BF16)
    halo_x[...] = jnp.zeros_like(halo_x)
    halo_b[...] = jnp.zeros_like(halo_b)
    for load in loads:
        load.wait()

    arrive(order[1])
    near(order[0], True)
    arrive(order[2])
    last(order[0], True)
    near(order[1], False)
    arrive(order[3])
    project(order[0], True)
    arrive_early(order[2])
    arrive_early(order[1])
    near(order[2], False)
    last(order[1], False)
    gates(order[0])
    arrive_early(order[3])
    near(order[3], False)
    project(order[1], False)
    pass_bc(order[0])
    last(order[2], False)
    gates(order[1])
    project(order[2], False)
    pass_bc(order[1])
    last(order[3], False)
    gates(order[2])
    pass_bc(order[2])
    project(order[3], False)
    pass_bc(order[3])

    row = lax.broadcasted_iota(jnp.int32, (8, 128), 0)
    bias_col = jnp.zeros((8, 128), F32)
    rate_col = jnp.zeros((8, 128), F32)
    for k in range(HEADS):
        bias_col = jnp.where(row == k, bias[k], bias_col)
        rate_col = jnp.where(row == k, alog[k], rate_col)
    rate_col = jnp.exp(rate_col)
    upper = (lax.broadcasted_iota(jnp.int32, (128, 128), 0)
             <= lax.broadcasted_iota(jnp.int32, (128, 128), 1))
    parts = []
    for b in range(8):
        v = dt[0:8, b * 128:(b + 1) * 128] + bias_col
        v = jnp.maximum(v, 0.0) + jnp.log1p(jnp.exp(-jnp.abs(v)))
        step[b * 8:(b + 1) * 8, :] = v
        parts.append(-v * rate_col)
    dec = jnp.concatenate(parts, axis=0)
    cum = jnp.dot(dec, upper.astype(F32), preferred_element_type=F32, precision=lax.Precision.HIGHEST)
    cums[...] = cum
    tot = jnp.broadcast_to(cum[:, 127:128], (64, 128))
    weight = step[...] * jnp.exp(tot - cum)
    cumt[...] = (cum - jnp.log(step[...])).T

    lane = lax.broadcasted_iota(jnp.int32, (64, 128), 1)
    tapx = jnp.concatenate([cx[...], jnp.zeros((4, W), F32)], axis=0).T

    def conv(src, r0, taps, hrow, dst, first, count):
        prev = hpad[hrow:hrow + 64, :] if first == 0 else src[r0:r0 + 64, (first - 1) * 128:first * 128].astype(F32)
        for b in range(first, first + count):
            cur = src[r0:r0 + 64, b * 128:(b + 1) * 128].astype(F32)
            total = taps[:, 3:4] * cur
            for k in range(1, 4):
                moved = pltpu.roll(jnp.where(lane >= 128 - k, prev, cur), k, 1)
                total = total + taps[:, 3 - k:4 - k] * moved
            dst[r0:r0 + 64, b * 128:(b + 1) * 128] = silu(total).astype(BF16)
            prev = cur

    for k in range(HEADS):
        conv(pre, k * 64, tapx[k * 64:(k + 1) * 64], 0, xc, 1, 7)
    for p in range(4):
        share_wait(p, 0)
        share_wait(p, 2)
    for k in range(3):
        taps_wait(k)
    tapb = [taps[q].T[0:64] for q in range(4)]
    for q in range(4):
        conv(bcp, q * 64, tapb[q], 0, bcf, 1, 7)

    @pl.when(s == 0)
    def _():
        hpad[...] = jnp.zeros_like(hpad)

    @pl.when(s > 0)
    def _():
        rcopy(halo_x, in_x, hxs, hxr, seq=s).wait_recv()
        hpad[0:W, :] = lax.dot_general(in_x[:, 0:W], pick, TN, preferred_element_type=F32)
        for q in range(4):
            rcopy(halo_b, in_b.at[q], hbs.at[0], hbr.at[q], seq=s).wait_recv()
            hpad[W + q * 64:W + q * 64 + 64, :] = lax.dot_general(
                in_b[q, :, 0:64], pick, TN, preferred_element_type=F32)

    for k in range(HEADS):
        conv(pre, k * 64, tapx[k * 64:(k + 1) * 64], k * 64, xc, 0, 1)
    for q in range(4):
        conv(bcp, q * 64, tapb[q], W + q * 64, bcf, 0, 1)

    def rows(v, r):
        return jnp.concatenate(
            [jnp.broadcast_to(v[r + k:r + k + 1, :], (64, 128)) for k in range(HEADS)], axis=0)

    state = jnp.zeros((W, 128), F32)
    total = jnp.zeros((8, 128), F32)
    for b in range(8):
        cols = slice(b * 128, (b + 1) * 128)
        sstart[b] = state
        xw = (xc[:, cols].astype(F32) * rows(weight, b * 8)).astype(BF16)
        fresh = lax.dot_general(xw, bcf[0:128, cols], NT, preferred_element_type=F32)
        tb = tot[b * 8:(b + 1) * 8, :]
        state = state * rows(jnp.exp(tb), 0) + fresh
        total = total + tb
    sfin[...] = state.astype(BF16)
    tfin[...] = total
    for t in range(1, NSEQ):
        @pl.when(s + t < NSEQ)
        def _():
            rcopy(sfin, st_in.at[s], ss.at[t], sr.at[s], seq=s + t).start()
            rcopy(tfin, tot_in.at[s], ts.at[t], tr.at[s], seq=s + t).start()

    gates(order[3])
    for b in range(8):
        cols = slice(b * 128, (b + 1) * 128)
        scores = lax.dot_general(bcf[0:128, cols], bcf[128:256, cols], TN, preferred_element_type=F32)
        scores = jnp.where(upper, scores, 0.0)
        for k in range(HEADS):
            r = b * 8 + k
            diff = cums[r:r + 1, :] - cumt[:, r:r + 1]
            mixing = jnp.exp(jnp.where(upper, diff, -jnp.inf)) * scores
            yin[k * 64:(k + 1) * 64, cols] = jnp.dot(
                xc[k * 64:(k + 1) * 64, cols], mixing.astype(BF16), preferred_element_type=F32)

    inc[...] = jnp.zeros_like(inc)
    for q in range(NSEQ - 1):
        @pl.when(q < s)
        def _():
            rcopy(sfin, st_in.at[q], ss.at[0], sr.at[q], seq=s).wait_recv()
            rcopy(tfin, tot_in.at[q], ts.at[0], tr.at[q], seq=s).wait_recv()
            inc[...] = inc[...] * rows(jnp.exp(tot_in[q]), 0) + st_in[q].astype(F32)

    skips = jnp.concatenate([jnp.full((64, 128), skip[k], F32) for k in range(HEADS)], axis=0)
    offset = jnp.zeros((8, 128), F32)
    for b in range(8):
        cols = slice(b * 128, (b + 1) * 128)
        st = (sstart[b] + inc[...] * rows(jnp.exp(offset), 0)).astype(BF16)
        yst = jnp.dot(st, bcf[128:256, cols], preferred_element_type=F32)
        yv = yin[:, cols] + yst * rows(jnp.exp(cums[b * 8:(b + 1) * 8, :]), 0) + skips * xc[:, cols].astype(F32)
        yv = yv.astype(BF16).astype(F32)
        g = (yv * silu(pre[W:BB, cols].astype(F32))).T
        for i in range(4):
            sb[4 * b + i, :, 0:W] = g[32 * i:32 * i + 16, :].astype(BF16)
            sb[4 * b + i, :, W:BB] = g[32 * i + 16:32 * i + 32, :].astype(BF16)
        offset = offset + tot[b * 8:(b + 1) * 8, :]

    def scatter(k, _):
        dst = (h + 16 + k) % 32

        @pl.when(k != 16)
        def _():
            rcopy(sb.at[dst], rbuf.at[h], as_.at[dst], ar.at[h], head=dst).start()

        return 0

    lax.fori_loop(0, 32, scatter, 0)
    rbuf[h] = sb[h]

    def collect(k, _):
        src = (h + k) % 32
        rcopy(sb.at[src], rbuf.at[src], as_.at[src], ar.at[src], head=h).wait_recv()
        return 0

    lax.fori_loop(1, 32, collect, 0)

    for q in range(32):
        asm[0:16, q * W:(q + 1) * W] = rbuf[q, :, 0:W]
        asm[16:32, q * W:(q + 1) * W] = rbuf[q, :, W:BB]
    for g in range(5):
        v = asm[:, g * 2048:(g + 1) * 2048].astype(F32)
        scale = lax.rsqrt(jnp.mean(v * v, axis=1, keepdims=True) + 1e-5)
        for k in range(16):
            c0 = g * 16 + k
            out[:, c0 * 128:(c0 + 1) * 128] = (
                v[:, k * 128:(k + 1) * 128] * scale * gain[c0:c0 + 1, :]).astype(BF16)

    for k in range(3):
        taps_copy(k).wait_send()
    for j in range(4):
        p = order[j]
        for sign in (1, -1):
            along(p, sign, lambda d: d.wait_send())
            for yy in (left, right, far):
                along_early(p, yy, sign, lambda d: d.wait_send())
        for kind in range(4):
            ring(p, kind, j == 0).wait_send()
        twin(p, y, True).wait_send()
        for yy in (left, right, far):
            twin(p, yy, j == 0).wait_send()
            if j:
                twin_early(p, yy).wait_send()
        for kind in range(3):
            share_copy(p, kind).wait_send()

    @pl.when(s < NSEQ - 1)
    def _():
        for copy in halo_copies():
            copy.wait_send()

    for t in range(1, NSEQ):
        @pl.when(s + t < NSEQ)
        def _():
            rcopy(sfin, st_in.at[s], ss.at[t], sr.at[s], seq=s).wait_send()
            rcopy(tfin, tot_in.at[s], ts.at[t], tr.at[s], seq=s).wait_send()

    def sent(k, _):
        dst = (h + k) % 32
        rcopy(sb.at[dst], rbuf.at[h], as_.at[dst], ar.at[h], head=h).wait_send()
        return 0

    lax.fori_loop(1, 32, sent, 0)


def call(tok, wx, wz, wbc, wdt, cx, cbc, bias, alog, skip, gain):
    d = tok.shape[1]
    anywhere = pl.BlockSpec(memory_space=pl.ANY)
    vm = pl.BlockSpec(memory_space=pltpu.VMEM)
    sm = pl.BlockSpec(memory_space=pltpu.SMEM)
    dma = pltpu.SemaphoreType.DMA
    mem = pltpu.VMEM
    return pl.pallas_call(
        kernel,
        out_shape=jax.ShapeDtypeStruct((32, 10240), BF16),
        in_specs=[anywhere] * 4 + [vm] * 3 + [sm] * 3 + [vm],
        out_specs=vm,
        scratch_shapes=[
            mem((32, 32, d), BF16), mem((BB + 80, d), BF16), mem((BB + 80, 256), F32),
            mem((BB, 1024), BF16), mem((16, 1024), F32), mem((256, 1024), BF16), mem((256, 1024), BF16),
            mem((16, 384), BF16), mem((16, 128), BF16), mem((16, 384), BF16), mem((4, 16, 128), BF16),
            mem((W + 256, 128), F32), mem((4, 8, 128), F32), mem((W, 1024), BF16),
            mem((64, 128), F32), mem((64, 128), F32), mem((128, 64), F32), mem((W, 1024), F32),
            mem((8, W, 128), F32), mem((W, 128), BF16), mem((8, 128), F32),
            mem((8, W, 128), BF16), mem((8, 8, 128), F32), mem((W, 128), F32),
            mem((32, 16, BB), BF16), mem((32, 16, BB), BF16), mem((32, 10240), BF16),
            dma((4,)), dma((4, 2)), dma((4,)), dma((4, 4, 2)), dma((4, 4)),
            dma((4, 4)), dma((4, 4)), dma((4, 4)), dma((4, 4)), dma((4, 4)), dma((4, 4)),
            dma((4, 3)), dma((4, 3)), dma((3,)), dma((4,)), dma, dma, dma((4,)), dma((4,)),
            dma((8,)), dma((8,)), dma((8,)), dma((8,)), dma((32,)), dma((32,)),
        ],
        compiler_params=pltpu.CompilerParams(collective_id=0, has_side_effects=True,
                                             vmem_limit_bytes=60 * 2**20),
        name="mixer",
    )(tok, wx, wz, wbc, wdt, cx, cbc, bias, alog, skip, gain.reshape(80, 128))


def shards(tokens, wx, wz, wbc, wdt, cx, cbc, bias, alog, skip, gain):
    return call(tokens, wx.T, wz.T, wbc.T, wdt.T, cx, cbc, bias, alog, skip, gain)


def solution(mesh):
    cols = P(None, "head")
    placed = (P(("seq", "head"), None), cols, cols, cols, cols, cols, cols,
              P("head"), P("head"), P("head"), P())
    return jax.shard_map(
        shards, mesh=mesh, in_specs=placed, out_specs=P(("seq", "head"), None), check_vma=False
    )
```

time: 143 us -> 125 us (0.87)
  the two profiles are of different devices: /device:TPU:255 before, /device:TPU:7 now
where the time goes in v2:
time: 125 us; the launch traced here: 123 us
  Pallas kernels  121 us (97%)
  local copies, waits for them, and re-layouts  1.97 us (2%)
    pallas_call x1, Pallas kernels, call(): pl.pallas_call(kernel, out_shape=jax.ShapeDtypeStruct((32, 10240), BF16),...  121 us

profile of v2, /device:TPU:7, one launch (start us, length us, event | category | flops | bytes accessed | tf_op | source)
XLA Modules:
  0.0 122.9 jit_solution(14286364359812149662)
XLA Ops:
  0.0 120.9 %mixer.1 = bf16[32,10240]{1,0:T(8,128)(2,1)} custom-call(bf16[32,8192]{1,0:T(8,128)(2,1)} %tok.1, bf16[320,8192]{1,0:T(8,128)(2,1)} %bitcast.5, bf16[320,8192]{1,0:T(8,128)(2,1)} %bitcast.6, bf16[64,8192]{1,0:T(8,128)(2,1)} %bitcast.7, bf16[5,8192]{1,0:T(8,128)(2,1)} %bitcast.8, f32[4,320]{1,0:T(4,128)} %cx.1, f32[4,64]{1,0:T(4,128)} %cbc.1, f32[5]{0:T(128)} %bias.1, ...), custom_call_target="tpu_custom_call" | custom-call | tf_op jit(solution)/shard_map/mixer/pallas_call | solution.py:508
  120.9 2.0 %copy.13 = bf16[32,10240]{1,0:T(8,128)(2,1)} copy(bf16[32,10240]{1,0:T(8,128)(2,1)} %mixer.1) | data formatting | bytes 1310720

commit v3 on v2

--- a/solution.py
+++ b/solution.py
@@ -11,7 +11,7 @@
 NT = (((1,), (1,)), ((), ()))
 TN = (((0,), (0,)), ((), ()))
 KC = 4096
-EARLY = 1536
+EARLY = 3328
 HEADS = 5
 W = 320
 BB = 2 * W
@@ -32,9 +32,9 @@
 
 def kernel(tok, wx, wz, wbc, wdt, cx, cbc, bias, alog, skip, gain, out,
            buf, wt, res, pre, dt, bcp, bcf, halo_x, halo_b, in_x, in_b, hpad, taps, xc,
-           step, cums, cumt, yin, sstart, sfin, tfin, st_in, tot_in, inc, sb, rbuf, asm,
+           step, cums, cumt, yin, sstart, offs, sfin, tfin, st_mate, tot_mate, tail_s, tail_t, xfin, xtot, st_in, tot_in, inc, sb, rbuf, asm,
            lsem, zs, zr, es, er, ys, yr, ds, dr, fs, fr,
-           bs, br, cs, cr, hxs, hxr, hbs, hbr, ss, sr, ts, tr, as_, ar):
+           bs, br, cs, cr, hxs, hxr, hbs, hbr, ss, sr, ts, tr, xs, xr, vs, vr, as_, ar):
     h = lax.axis_index("head")
     s = lax.axis_index("seq")
     z, y, c = h // 8, (h // 2) % 4, h % 2
@@ -43,8 +43,27 @@
     across = h + 2 - 4 * (y % 2)
     base = (h // 4) * 4
     quarter = h % 4
-    zz = jnp.where(z < 2, z, 3 - z)
-    order = [jnp.where(z < 2, q, 3 - q) for q in (zz, 1 - zz, 2, 3)]
+    x, zh = s // 2, s % 2
+    place = zh * 4 + z
+    mate = s + 1 - 2 * zh
+    ends = jnp.logical_or(place < 2, place >= 6)
+    middle = jnp.logical_not(ends)
+    first_run = jnp.where(ends, (place + 3) % 8, 4)
+    turn = jnp.where(ends, 0, (place + 7) % 4)
+    order = [z, (z + 1) % 4, (z + 3) % 4, (z + 2) % 4]
+
+    def plane_in(slot):
+        return (place + 7 + (slot - z + 5) % 4) % 8
+
+    def owner(slot):
+        return x * 2 + plane_in(slot) // 4
+
+    def slot_of(k):
+        return (turn + k) % 4
+
+    def upward(dz):
+        there = (place + dz + 8) % 8
+        return dict(seq=x * 2 + there // 4, head=(there % 4) * 8 + y * 2 + c)
 
     def at(p, yy):
         return p * 8 + yy * 2 + c
@@ -58,50 +77,49 @@
     ]
     barrier = pltpu.get_barrier_semaphore()
 
+    def signal(**device):
+        pl.semaphore_signal(barrier, inc=1, device_id=device, device_id_type=MESH)
+
     def greet(k, _):
-        pl.semaphore_signal(barrier, inc=1, device_id={"head": (h + k) % 32}, device_id_type=MESH)
+        there = (place + 6 + k // 8) % 8
+        who = (there % 4) * 8 + k % 8
+
+        @pl.when(k != 16 + h % 8)
+        def _():
+            signal(seq=x * 2 + there // 4, head=who)
+
         return 0
 
-    def greet_seq(k, _):
-        pl.semaphore_signal(barrier, inc=1, device_id={"seq": (s + k) % NSEQ}, device_id_type=MESH)
-        return 0
-
-    lax.fori_loop(1, 32, greet, 0)
-    lax.fori_loop(1, NSEQ, greet_seq, 0)
-
-    @pl.when(s > 0)
-    def _():
-        for k in range(1, 4):
-            pl.semaphore_signal(barrier, inc=1, device_id={"seq": s - 1, "head": base + (h + k) % 4},
-                                device_id_type=MESH)
-
-    pl.semaphore_wait(barrier, 31 + NSEQ - 1 + 3 * (s < NSEQ - 1).astype(jnp.int32))
+    lax.fori_loop(0, 32, greet, 0)
+    for k in range(1, 4):
+        signal(seq=(s + 2 * k) % NSEQ)
+    for k in range(4):
+        signal(seq=mate, head=base + k)
+    joined = jnp.logical_and(z == 1, middle)
+    alone = jnp.logical_and(z == 1, ends)
+    hand_on = jnp.logical_and(x < 3, jnp.logical_not(alone))
+    next_seq = jnp.where(joined, mate + 2, s + 2)
+    prev_seq = jnp.where(alone, mate - 2, s - 2)
+
+    @pl.when(jnp.logical_and(x > 0, ends))
+    def _():
+        for k in range(4):
+            signal(seq=prev_seq, head=base + k)
+
+    hands_on = jnp.logical_and(hand_on, jnp.logical_or(ends, joined))
+    pl.semaphore_wait(barrier, 31 + 3 + 4 + 4 * hands_on.astype(jnp.int32))
     own.wait()
 
     early = pl.ds(0, EARLY)
     late = pl.ds(EARLY, buf.shape[2] - EARLY)
 
-    def along(p, sign, act):
-        toward = (p <= z) if sign > 0 else (p >= z)
-        room = (z < 3) if sign > 0 else (z > 0)
-
-        @pl.when(jnp.logical_and(toward, room))
-        def _():
-            slot = buf.at[at(p, y)]
-            act(rcopy(slot, slot, zs.at[p, (sign + 1) // 2], zr.at[p], head=at(z + sign, y)))
-
-    def along_early(p, yy, sign, act):
-        toward = (p <= z) if sign > 0 else (p >= z)
-        room = (z < 3) if sign > 0 else (z > 0)
-
-        @pl.when(jnp.logical_and(toward, room))
-        def _():
-            slot = buf.at[at(p, yy), :, early]
-            act(rcopy(slot, slot, es.at[p, yy, (sign + 1) // 2], er.at[p, yy], head=at(z + sign, y)))
-
-    def both(move, *where):
-        move(*where, 1, lambda d: d.start())
-        move(*where, -1, lambda d: d.start())
+    def along(p, sign):
+        slot = buf.at[at(p, y)]
+        return rcopy(slot, slot, zs.at[p, (sign + 1) // 2], zr.at[p], **upward(sign))
+
+    def along_early(p, yy, sign):
+        slot = buf.at[at(p, yy), :, early]
+        return rcopy(slot, slot, es.at[p, yy, (sign + 1) // 2], er.at[p, yy], **upward(sign))
 
     def ring(p, kind, own_plane):
         cols = pl.ds(0, buf.shape[2]) if own_plane else late
@@ -141,17 +159,21 @@
         ring(p, 1, own_plane).start()
         twin(p, y, True).start()
 
-    def arrive(p):
+    def arrive(j):
+        p = order[j]
         slot = buf.at[at(p, y)]
         rcopy(slot, slot, zs.at[p, 0], zr.at[p], head=h).wait_recv()
-        both(along, p)
+        if j == 1:
+            along(p, -1).start()
         begin(p, False)
 
-    def arrive_early(p):
+    def arrive_early(j):
+        p = order[j]
         for yy in (left, right, far):
             slot = buf.at[at(p, yy), :, early]
             rcopy(slot, slot, es.at[p, yy, 0], er.at[p, yy], head=h).wait_recv()
-            both(along_early, p, yy)
+            if j == 1:
+                along_early(p, yy, -1).start()
             twin_early(p, yy).start()
 
     def near(p, own_plane):
@@ -162,14 +184,16 @@
         for yy in (left, right):
             twin(p, yy, own_plane).start()
             if own_plane:
-                both(along_early, p, yy)
+                along_early(p, yy, -1).start()
+                along_early(p, yy, 1).start()
 
     def last(p, own_plane):
         ring_wait(p, 2, own_plane)
         ring_wait(p, 3, own_plane)
         twin(p, far, own_plane).start()
         if own_plane:
-            both(along_early, p, far)
+            along_early(p, far, -1).start()
+            along_early(p, far, 1).start()
 
     def complete(p, own_plane):
         twin_wait(p, y, True)
@@ -236,20 +260,30 @@
     pick = (lax.broadcasted_iota(jnp.int32, (16, 128), 1)
             == lax.broadcasted_iota(jnp.int32, (16, 128), 0) + 112).astype(BF16)
 
-    def halo_copies():
-        yield rcopy(halo_x, in_x, hxs, hxr, seq=s + 1)
+    def halo_copies(i):
+        if i == 0:
+            to, slot = jnp.where(joined, next_seq, mate), jnp.where(jnp.logical_or(ends, joined), 0, 1)
+        else:
+            to, slot = next_seq, 0
+        yield rcopy(halo_x.at[i], in_x.at[slot], hxs.at[i], hxr.at[slot], seq=to)
         for k in range(4):
-            yield rcopy(halo_b, in_b.at[quarter], hbs.at[k], hbr.at[quarter], seq=s + 1, head=base + k)
+            yield rcopy(halo_b.at[i], in_b.at[slot, quarter], hbs.at[i, k], hbr.at[slot, quarter],
+                        seq=to, head=base + k)
+
+    halo_when = (jnp.logical_or(jnp.logical_not(joined), x < 3), jnp.logical_and(ends, hand_on))
+    halo_slot = (order[3], 3)
 
     def send_halo(p):
-        @pl.when(jnp.logical_and(p == 3, s < NSEQ - 1))
-        def _():
-            tail = pl.ds(896, 128)
-            halo_x[:, 0:W] = lax.dot_general(pick, pre[0:W, tail], NT, preferred_element_type=F32).astype(BF16)
-            halo_b[:, 0:64] = lax.dot_general(
-                pick, bcp[quarter_rows(quarter), tail], NT, preferred_element_type=F32).astype(BF16)
-            for copy in halo_copies():
-                copy.start()
+        for i in range(2):
+            @pl.when(jnp.logical_and(p == halo_slot[i], halo_when[i]))
+            def _():
+                tail = pl.ds(pl.multiple_of(p * 256 + 128, 128), 128)
+                halo_x[i, :, 0:W] = lax.dot_general(
+                    pick, pre[0:W, tail], NT, preferred_element_type=F32).astype(BF16)
+                halo_b[i, :, 0:64] = lax.dot_general(
+                    pick, bcp[quarter_rows(quarter), tail], NT, preferred_element_type=F32).astype(BF16)
+                for copy in halo_copies(i):
+                    copy.start()
 
     def project(p, own_plane):
         complete(p, own_plane)
@@ -270,7 +304,8 @@
         q = (h + k + 1) % 4
         rcopy(taps.at[q], taps.at[q], cs.at[k], cr.at[q], head=h).wait_recv()
 
-    both(along, order[0])
+    along(order[0], -1).start()
+    along(order[0], 1).start()
     begin(order[0], True)
     for load in loads:
         load.start()
@@ -284,31 +319,32 @@
     for load in loads:
         load.wait()
 
-    arrive(order[1])
+    arrive(1)
     near(order[0], True)
-    arrive(order[2])
+    arrive(2)
     last(order[0], True)
     near(order[1], False)
-    arrive(order[3])
     project(order[0], True)
-    arrive_early(order[2])
-    arrive_early(order[1])
+    arrive_early(2)
     near(order[2], False)
     last(order[1], False)
+    arrive_early(1)
+    arrive(3)
     gates(order[0])
-    arrive_early(order[3])
+    last(order[2], False)
+    project(order[1], False)
+    gates(order[1])
     near(order[3], False)
-    project(order[1], False)
+    project(order[2], False)
     pass_bc(order[0])
-    last(order[2], False)
-    gates(order[1])
-    project(order[2], False)
+    arrive_early(3)
+    last(order[3], False)
     pass_bc(order[1])
-    last(order[3], False)
-    gates(order[2])
     pass_bc(order[2])
     project(order[3], False)
-    pass_bc(order[3])
+
+    def cols_of(b):
+        return pl.ds(pl.multiple_of(slot_of(b // 2) * 256 + (b % 2) * 128, 128), 128)
 
     row = lax.broadcasted_iota(jnp.int32, (8, 128), 0)
     bias_col = jnp.zeros((8, 128), F32)
@@ -321,7 +357,7 @@
              <= lax.broadcasted_iota(jnp.int32, (128, 128), 1))
     parts = []
     for b in range(8):
-        v = dt[0:8, b * 128:(b + 1) * 128] + bias_col
+        v = dt[0:8, cols_of(b)] + bias_col
         v = jnp.maximum(v, 0.0) + jnp.log1p(jnp.exp(-jnp.abs(v)))
         step[b * 8:(b + 1) * 8, :] = v
         parts.append(-v * rate_col)
@@ -335,67 +371,107 @@
     lane = lax.broadcasted_iota(jnp.int32, (64, 128), 1)
     tapx = jnp.concatenate([cx[...], jnp.zeros((4, W), F32)], axis=0).T
 
-    def conv(src, r0, taps, hrow, dst, first, count):
-        prev = hpad[hrow:hrow + 64, :] if first == 0 else src[r0:r0 + 64, (first - 1) * 128:first * 128].astype(F32)
-        for b in range(first, first + count):
-            cur = src[r0:r0 + 64, b * 128:(b + 1) * 128].astype(F32)
-            total = taps[:, 3:4] * cur
-            for k in range(1, 4):
-                moved = pltpu.roll(jnp.where(lane >= 128 - k, prev, cur), k, 1)
-                total = total + taps[:, 3 - k:4 - k] * moved
-            dst[r0:r0 + 64, b * 128:(b + 1) * 128] = silu(total).astype(BF16)
-            prev = cur
+    def conv_block(src, r0, taps, prev, b, dst, to):
+        cur = src[r0:r0 + 64, cols_of(b)].astype(F32)
+        total = taps[:, 3:4] * cur
+        for k in range(1, 4):
+            moved = pltpu.roll(jnp.where(lane >= 128 - k, prev, cur), k, 1)
+            total = total + taps[:, 3 - k:4 - k] * moved
+        dst[r0:r0 + 64, to] = silu(total).astype(BF16)
+        return cur
+
+    def conv(src, r0, taps, dst):
+        prev = src[r0:r0 + 64, cols_of(0)].astype(F32)
+        for b in range(1, 8):
+            prev = conv_block(src, r0, taps, prev, b, dst, slice(b * 128, (b + 1) * 128))
 
     for k in range(HEADS):
-        conv(pre, k * 64, tapx[k * 64:(k + 1) * 64], 0, xc, 1, 7)
+        conv(pre, k * 64, tapx[k * 64:(k + 1) * 64], xc)
+    gates(order[2])
+    pass_bc(order[3])
+    for k in range(3):
+        taps_wait(k)
+    tapb = [taps[q].T[0:64] for q in range(4)]
     for p in range(4):
         share_wait(p, 0)
         share_wait(p, 2)
-    for k in range(3):
-        taps_wait(k)
-    tapb = [taps[q].T[0:64] for q in range(4)]
     for q in range(4):
-        conv(bcp, q * 64, tapb[q], 0, bcf, 1, 7)
-
-    @pl.when(s == 0)
-    def _():
-        hpad[...] = jnp.zeros_like(hpad)
-
-    @pl.when(s > 0)
-    def _():
-        rcopy(halo_x, in_x, hxs, hxr, seq=s).wait_recv()
-        hpad[0:W, :] = lax.dot_general(in_x[:, 0:W], pick, TN, preferred_element_type=F32)
+        conv(bcp, q * 64, tapb[q], bcf)
+
+    def starts(i, b):
+        to = pl.ds(pl.multiple_of(b * 128, 128), 128)
+        for k in range(HEADS):
+            conv_block(pre, k * 64, tapx[k * 64:(k + 1) * 64], hpad[i, k * 64:(k + 1) * 64, :], b, xc, to)
         for q in range(4):
-            rcopy(halo_b, in_b.at[q], hbs.at[0], hbr.at[q], seq=s).wait_recv()
-            hpad[W + q * 64:W + q * 64 + 64, :] = lax.dot_general(
-                in_b[q, :, 0:64], pick, TN, preferred_element_type=F32)
-
-    for k in range(HEADS):
-        conv(pre, k * 64, tapx[k * 64:(k + 1) * 64], k * 64, xc, 0, 1)
-    for q in range(4):
-        conv(bcp, q * 64, tapb[q], W + q * 64, bcf, 0, 1)
+            conv_block(bcp, q * 64, tapb[q], hpad[i, W + q * 64:W + (q + 1) * 64, :], b, bcf, to)
+
+    halo_due = (jnp.logical_or(middle, x > 0), jnp.logical_and(ends, z != 1))
+    hpad[0] = jnp.zeros((W + 256, 128), F32)
+    for i in range(2):
+        @pl.when(halo_due[i])
+        def _():
+            rcopy(halo_x.at[i], in_x.at[i], hxs.at[i], hxr.at[i], seq=s).wait_recv()
+            hpad[i, 0:W, :] = lax.dot_general(in_x[i, :, 0:W], pick, TN, preferred_element_type=F32)
+            for q in range(4):
+                rcopy(halo_b.at[i], in_b.at[i, q], hbs.at[i, 0], hbr.at[i, q], seq=s).wait_recv()
+                hpad[i, W + q * 64:W + q * 64 + 64, :] = lax.dot_general(
+                    in_b[i, q, :, 0:64], pick, TN, preferred_element_type=F32)
+            if i:
+                starts(1, 2 * first_run)
+
+    starts(0, 0)
 
     def rows(v, r):
         return jnp.concatenate(
             [jnp.broadcast_to(v[r + k:r + k + 1, :], (64, 128)) for k in range(HEADS)], axis=0)
 
+    def mate_copy(i):
+        return rcopy(sfin.at[i], st_mate.at[i], ss.at[i], sr.at[i], seq=mate)
+
+    def mate_total(i):
+        return rcopy(tfin.at[i], tot_mate.at[i], ts.at[i], tr.at[i], seq=mate)
+
     state = jnp.zeros((W, 128), F32)
     total = jnp.zeros((8, 128), F32)
-    for b in range(8):
-        cols = slice(b * 128, (b + 1) * 128)
-        sstart[b] = state
-        xw = (xc[:, cols].astype(F32) * rows(weight, b * 8)).astype(BF16)
-        fresh = lax.dot_general(xw, bcf[0:128, cols], NT, preferred_element_type=F32)
-        tb = tot[b * 8:(b + 1) * 8, :]
-        state = state * rows(jnp.exp(tb), 0) + fresh
-        total = total + tb
-    sfin[...] = state.astype(BF16)
-    tfin[...] = total
-    for t in range(1, NSEQ):
-        @pl.when(s + t < NSEQ)
-        def _():
-            rcopy(sfin, st_in.at[s], ss.at[t], sr.at[s], seq=s + t).start()
-            rcopy(tfin, tot_in.at[s], ts.at[t], tr.at[s], seq=s + t).start()
+    for k in range(4):
+        if k:
+            @pl.when(first_run == k)
+            def _():
+                sfin[0] = state.astype(BF16)
+                tfin[0] = total
+                mate_copy(0).start()
+                mate_total(0).start()
+
+            state = jnp.where(first_run == k, 0.0, state)
+            total = jnp.where(first_run == k, 0.0, total)
+        for b in (2 * k, 2 * k + 1):
+            cols = slice(b * 128, (b + 1) * 128)
+            sstart[b] = state
+            offs[b] = total
+            xw = (xc[:, cols].astype(F32) * rows(weight, b * 8)).astype(BF16)
+            fresh = lax.dot_general(xw, bcf[0:128, cols], NT, preferred_element_type=F32)
+            tb = tot[b * 8:(b + 1) * 8, :]
+            state = state * rows(jnp.exp(tb), 0) + fresh
+            total = total + tb
+
+    @pl.when(first_run == 4)
+    def _():
+        sfin[0] = state.astype(BF16)
+        tfin[0] = total
+        mate_copy(0).start()
+        mate_total(0).start()
+        sfin[1] = jnp.zeros((W, 128), BF16)
+        tfin[1] = jnp.zeros((8, 128), F32)
+
+    @pl.when(first_run < 4)
+    def _():
+        sfin[1] = state.astype(BF16)
+        tfin[1] = total
+
+    @pl.when(ends)
+    def _():
+        mate_copy(1).start()
+        mate_total(1).start()
 
     gates(order[3])
     for b in range(8):
@@ -409,34 +485,75 @@
             yin[k * 64:(k + 1) * 64, cols] = jnp.dot(
                 xc[k * 64:(k + 1) * 64, cols], mixing.astype(BF16), preferred_element_type=F32)
 
-    inc[...] = jnp.zeros_like(inc)
-    for q in range(NSEQ - 1):
-        @pl.when(q < s)
+    mate_copy(0).wait_recv()
+    mate_total(0).wait_recv()
+
+    @pl.when(middle)
+    def _():
+        mate_copy(1).wait_recv()
+        mate_total(1).wait_recv()
+
+    def grown(v, t):
+        return v * rows(jnp.exp(t), 0)
+
+    head_s = jnp.where(ends, sfin[0].astype(F32), st_mate[0].astype(F32))
+    head_t = jnp.where(ends, tfin[0], tot_mate[0])
+    mid_s = jnp.where(ends, st_mate[0].astype(F32), sfin[0].astype(F32))
+    mid_t = jnp.where(ends, tot_mate[0], tfin[0])
+
+    @pl.when(middle)
+    def _():
+        tail_s[...] = st_mate[1].astype(F32)
+        tail_t[...] = tot_mate[1]
+
+    @pl.when(ends)
+    def _():
+        tail_s[...] = sfin[1].astype(F32)
+        tail_t[...] = tfin[1]
+
+    xfin[...] = (grown(grown(head_s, mid_t) + mid_s, tail_t[...]) + tail_s[...]).astype(BF16)
+    xtot[...] = head_t + mid_t + tail_t[...]
+    for t in range(1, 4):
+        @pl.when(x + t < 4)
         def _():
-            rcopy(sfin, st_in.at[q], ss.at[0], sr.at[q], seq=s).wait_recv()
-            rcopy(tfin, tot_in.at[q], ts.at[0], tr.at[q], seq=s).wait_recv()
-            inc[...] = inc[...] * rows(jnp.exp(tot_in[q]), 0) + st_in[q].astype(F32)
+            rcopy(xfin, st_in.at[x], xs.at[t], xr.at[x], seq=s + 2 * t).start()
+            rcopy(xtot, tot_in.at[x], vs.at[t], vr.at[x], seq=s + 2 * t).start()
+
+    inc[0] = jnp.zeros((W, 128), F32)
+    for q in range(3):
+        @pl.when(q < x)
+        def _():
+            rcopy(xfin, st_in.at[q], xs.at[0], xr.at[q], seq=s).wait_recv()
+            rcopy(xtot, tot_in.at[q], vs.at[0], vr.at[q], seq=s).wait_recv()
+            inc[0] = grown(inc[0], tot_in[q]) + st_in[q].astype(F32)
+
+    after_head = grown(inc[0], head_t) + head_s
+    inc[1] = grown(after_head, mid_t) + mid_s
+
+    @pl.when(middle)
+    def _():
+        inc[0] = after_head
 
     skips = jnp.concatenate([jnp.full((64, 128), skip[k], F32) for k in range(HEADS)], axis=0)
-    offset = jnp.zeros((8, 128), F32)
     for b in range(8):
         cols = slice(b * 128, (b + 1) * 128)
-        st = (sstart[b] + inc[...] * rows(jnp.exp(offset), 0)).astype(BF16)
+        run = jnp.where(first_run <= b // 2, 1, 0)
+        st = (sstart[b] + inc[run] * rows(jnp.exp(offs[b]), 0)).astype(BF16)
         yst = jnp.dot(st, bcf[128:256, cols], preferred_element_type=F32)
         yv = yin[:, cols] + yst * rows(jnp.exp(cums[b * 8:(b + 1) * 8, :]), 0) + skips * xc[:, cols].astype(F32)
         yv = yv.astype(BF16).astype(F32)
-        g = (yv * silu(pre[W:BB, cols].astype(F32))).T
+        g = (yv * silu(pre[W:BB, cols_of(b)].astype(F32))).T
         for i in range(4):
-            sb[4 * b + i, :, 0:W] = g[32 * i:32 * i + 16, :].astype(BF16)
-            sb[4 * b + i, :, W:BB] = g[32 * i + 16:32 * i + 32, :].astype(BF16)
-        offset = offset + tot[b * 8:(b + 1) * 8, :]
+            dst = slot_of(b // 2) * 8 + 4 * (b % 2) + i
+            sb[dst, :, 0:W] = g[32 * i:32 * i + 16, :].astype(BF16)
+            sb[dst, :, W:BB] = g[32 * i + 16:32 * i + 32, :].astype(BF16)
 
     def scatter(k, _):
         dst = (h + 16 + k) % 32
 
         @pl.when(k != 16)
         def _():
-            rcopy(sb.at[dst], rbuf.at[h], as_.at[dst], ar.at[h], head=dst).start()
+            rcopy(sb.at[dst], rbuf.at[h], as_.at[dst], ar.at[h], seq=owner(dst // 8), head=dst).start()
 
         return 0
 
@@ -465,10 +582,10 @@
         taps_copy(k).wait_send()
     for j in range(4):
         p = order[j]
-        for sign in (1, -1):
-            along(p, sign, lambda d: d.wait_send())
+        for sign in (-1, 1)[:2 if j == 0 else 1 if j == 1 else 0]:
+            along(p, sign).wait_send()
             for yy in (left, right, far):
-                along_early(p, yy, sign, lambda d: d.wait_send())
+                along_early(p, yy, sign).wait_send()
         for kind in range(4):
             ring(p, kind, j == 0).wait_send()
         twin(p, y, True).wait_send()
@@ -479,16 +596,25 @@
         for kind in range(3):
             share_copy(p, kind).wait_send()
 
-    @pl.when(s < NSEQ - 1)
-    def _():
-        for copy in halo_copies():
-            copy.wait_send()
-
-    for t in range(1, NSEQ):
-        @pl.when(s + t < NSEQ)
+    for i in range(2):
+        @pl.when(halo_when[i])
         def _():
-            rcopy(sfin, st_in.at[s], ss.at[t], sr.at[s], seq=s).wait_send()
-            rcopy(tfin, tot_in.at[s], ts.at[t], tr.at[s], seq=s).wait_send()
+            for copy in halo_copies(i):
+                copy.wait_send()
+
+    mate_copy(0).wait_send()
+    mate_total(0).wait_send()
+
+    @pl.when(ends)
+    def _():
+        mate_copy(1).wait_send()
+        mate_total(1).wait_send()
+
+    for t in range(1, 4):
+        @pl.when(x + t < 4)
+        def _():
+            rcopy(xfin, st_in.at[x], xs.at[t], xr.at[x], seq=s).wait_send()
+            rcopy(xtot, tot_in.at[x], vs.at[t], vr.at[x], seq=s).wait_send()
 
     def sent(k, _):
         dst = (h + k) % 32
@@ -513,16 +639,19 @@
         scratch_shapes=[
             mem((32, 32, d), BF16), mem((BB + 80, d), BF16), mem((BB + 80, 256), F32),
             mem((BB, 1024), BF16), mem((16, 1024), F32), mem((256, 1024), BF16), mem((256, 1024), BF16),
-            mem((16, 384), BF16), mem((16, 128), BF16), mem((16, 384), BF16), mem((4, 16, 128), BF16),
-            mem((W + 256, 128), F32), mem((4, 8, 128), F32), mem((W, 1024), BF16),
+            mem((2, 16, 384), BF16), mem((2, 16, 128), BF16), mem((2, 16, 384), BF16), mem((2, 4, 16, 128), BF16),
+            mem((2, W + 256, 128), F32), mem((4, 8, 128), F32), mem((W, 1024), BF16),
             mem((64, 128), F32), mem((64, 128), F32), mem((128, 64), F32), mem((W, 1024), F32),
-            mem((8, W, 128), F32), mem((W, 128), BF16), mem((8, 128), F32),
-            mem((8, W, 128), BF16), mem((8, 8, 128), F32), mem((W, 128), F32),
+            mem((8, W, 128), F32), mem((8, 8, 128), F32), mem((2, W, 128), BF16), mem((2, 8, 128), F32),
+            mem((2, W, 128), BF16), mem((2, 8, 128), F32), mem((W, 128), F32), mem((8, 128), F32),
+            mem((W, 128), BF16), mem((8, 128), F32),
+            mem((3, W, 128), BF16), mem((3, 8, 128), F32), mem((2, W, 128), F32),
             mem((32, 16, BB), BF16), mem((32, 16, BB), BF16), mem((32, 10240), BF16),
             dma((4,)), dma((4, 2)), dma((4,)), dma((4, 4, 2)), dma((4, 4)),
             dma((4, 4)), dma((4, 4)), dma((4, 4)), dma((4, 4)), dma((4, 4)), dma((4, 4)),
-            dma((4, 3)), dma((4, 3)), dma((3,)), dma((4,)), dma, dma, dma((4,)), dma((4,)),
-            dma((8,)), dma((8,)), dma((8,)), dma((8,)), dma((32,)), dma((32,)),
+            dma((4, 3)), dma((4, 3)), dma((3,)), dma((4,)), dma((2,)), dma((2,)), dma((2, 4)), dma((2, 4)),
+            dma((2,)), dma((2,)), dma((2,)), dma((2,)), dma((4,)), dma((3,)), dma((4,)), dma((3,)),
+            dma((32,)), dma((32,)),
         ],
         compiler_params=pltpu.CompilerParams(collective_id=0, has_side_effects=True,
                                              vmem_limit_bytes=60 * 2**20),

time: 125 us -> 110 us (0.88); the launches traced: 123 us -> 110 us
  Pallas kernels: 121 us -> 108 us
    pallas_call x1, Pallas kernels: 121 us -> 108 us  [call(): pl.pallas_call(kernel, out_shape=jax.ShapeDtypeStruct((32, 10240), BF16),...]
where the time goes in v3:
time: 110 us
  Pallas kernels  108 us (98%)
  local copies, waits for them, and re-layouts  1.97 us (2%)
    pallas_call x1, Pallas kernels, call(): pl.pallas_call(kernel, out_shape=jax.ShapeDtypeStruct((32, 10240), BF16),...  108 us

profile of v3, /device:TPU:7, one launch (start us, length us, event | category | flops | bytes accessed | tf_op | source)
XLA Modules:
  0.0 110.3 jit_solution(8535335405139850658)
XLA Ops:
  0.0 108.3 %mixer.1 = bf16[32,10240]{1,0:T(8,128)(2,1)} custom-call(bf16[32,8192]{1,0:T(8,128)(2,1)} %tok.1, bf16[320,8192]{1,0:T(8,128)(2,1)} %bitcast.5, bf16[320,8192]{1,0:T(8,128)(2,1)} %bitcast.6, bf16[64,8192]{1,0:T(8,128)(2,1)} %bitcast.7, bf16[5,8192]{1,0:T(8,128)(2,1)} %bitcast.8, f32[4,320]{1,0:T(4,128)} %cx.1, f32[4,64]{1,0:T(4,128)} %cbc.1, f32[5]{0:T(128)} %bias.1, ...), custom_call_target="tpu_custom_call" | custom-call | tf_op jit(solution)/shard_map/mixer/pallas_call | solution.py:634
  108.3 2.0 %copy.13 = bf16[32,10240]{1,0:T(8,128)(2,1)} copy(bf16[32,10240]{1,0:T(8,128)(2,1)} %mixer.1) | data formatting | bytes 1310720

commit v4 on v3

--- a/solution.py
+++ b/solution.py
@@ -11,7 +11,7 @@
 NT = (((1,), (1,)), ((), ()))
 TN = (((0,), (0,)), ((), ()))
 KC = 4096
-EARLY = 3328
+EARLY = 3072
 HEADS = 5
 W = 320
 BB = 2 * W
@@ -30,9 +30,9 @@
     return v / (1.0 + jnp.exp(-v))
 
 
-def kernel(tok, wx, wz, wbc, wdt, cx, cbc, bias, alog, skip, gain, out,
-           buf, wt, res, pre, dt, bcp, bcf, halo_x, halo_b, in_x, in_b, hpad, taps, xc,
-           step, cums, cumt, yin, sstart, offs, sfin, tfin, st_mate, tot_mate, tail_s, tail_t, xfin, xtot, st_in, tot_in, inc, sb, rbuf, asm,
+def kernel(tok, wx, wz, wbc, wdt, cx, cbc, bias, alog, skip, rbuf,
+           wdt_v, cx_v, cbc_v, buf, wt, res, pre, dt, bcp, bcf, halo_x, halo_b, in_x, in_b, hpad, taps, xc,
+           step, cums, cumt, yin, sstart, offs, sfin, tfin, st_mate, tot_mate, own_s, xfin, xtot, st_in, tot_in, inc, sb,
            lsem, zs, zr, es, er, ys, yr, ds, dr, fs, fr,
            bs, br, cs, cr, hxs, hxr, hbs, hbr, ss, sr, ts, tr, xs, xr, vs, vr, as_, ar):
     h = lax.axis_index("head")
@@ -75,6 +75,8 @@
         pltpu.make_async_copy(wz, wt.at[pl.ds(FIRST, W)], lsem.at[2]),
         pltpu.make_async_copy(wbc, wt.at[pl.ds(W, 64)], lsem.at[3]),
     ]
+    smalls = [pltpu.make_async_copy(src, dst, lsem.at[4 + i])
+              for i, (src, dst) in enumerate(((wdt, wdt_v), (cx, cx_v), (cbc, cbc_v)))]
     barrier = pltpu.get_barrier_semaphore()
 
     def signal(**device):
@@ -108,14 +110,12 @@
 
     hands_on = jnp.logical_and(hand_on, jnp.logical_or(ends, joined))
     pl.semaphore_wait(barrier, 31 + 3 + 4 + 4 * hands_on.astype(jnp.int32))
-    own.wait()
-
     early = pl.ds(0, EARLY)
     late = pl.ds(EARLY, buf.shape[2] - EARLY)
 
-    def along(p, sign):
+    def along(p, sign, own_plane):
         slot = buf.at[at(p, y)]
-        return rcopy(slot, slot, zs.at[p, (sign + 1) // 2], zr.at[p], **upward(sign))
+        return rcopy(tok if own_plane else slot, slot, zs.at[p, (sign + 1) // 2], zr.at[p], **upward(sign))
 
     def along_early(p, yy, sign):
         slot = buf.at[at(p, yy), :, early]
@@ -128,7 +128,8 @@
             (left, pl.ds(0, 16), right), (right, pl.ds(16, 16), left),
         )[kind]
         part = buf.at[at(p, yy), rows, cols]
-        return rcopy(part, part, ys.at[p, kind], yr.at[p, kind], head=at(z, to))
+        src = tok if own_plane and kind < 2 else part
+        return rcopy(src, part, ys.at[p, kind], yr.at[p, kind], head=at(z, to))
 
     def ring_wait(p, kind, own_plane):
         cols = pl.ds(0, buf.shape[2]) if own_plane else late
@@ -137,9 +138,9 @@
         part = buf.at[at(p, yy), rows, cols]
         rcopy(part, part, ys.at[p, kind], yr.at[p, kind], head=h).wait_recv()
 
-    def twin(p, yy, whole):
+    def twin(p, yy, whole, mine=False):
         slot = buf.at[at(p, yy)] if whole else buf.at[at(p, yy), :, late]
-        return rcopy(slot, slot, ds.at[p, yy], dr.at[p, yy], head=sib)
+        return rcopy(tok if mine else slot, slot, ds.at[p, yy], dr.at[p, yy], head=sib)
 
     def twin_wait(p, yy, whole):
         slot = buf.at[p * 8 + yy * 2 + 1 - c]
@@ -157,14 +158,14 @@
     def begin(p, own_plane):
         ring(p, 0, own_plane).start()
         ring(p, 1, own_plane).start()
-        twin(p, y, True).start()
+        twin(p, y, True, own_plane).start()
 
     def arrive(j):
         p = order[j]
         slot = buf.at[at(p, y)]
         rcopy(slot, slot, zs.at[p, 0], zr.at[p], head=h).wait_recv()
         if j == 1:
-            along(p, -1).start()
+            along(p, -1, False).start()
         begin(p, False)
 
     def arrive_early(j):
@@ -195,30 +196,28 @@
             along_early(p, far, -1).start()
             along_early(p, far, 1).start()
 
-    def complete(p, own_plane):
+    def complete_early(p):
         twin_wait(p, y, True)
         for yy in (left, right, far):
-            twin_wait(p, yy, own_plane)
-            if not own_plane:
-                twin_early_wait(p, yy)
-
-    def product(p, r0, n):
-        def chunk(k, _):
-            ks = pl.ds(pl.multiple_of(k * KC, KC), KC)
-            a = buf[pl.ds(p * 8, 8), :, ks].reshape(256, KC)
-            part = lax.dot_general(wt[r0:r0 + n, ks], a, NT, preferred_element_type=F32)
-
-            @pl.when(k == 0)
-            def _():
-                res[r0:r0 + n] = part
-
-            @pl.when(k > 0)
-            def _():
-                res[r0:r0 + n] += part
-
-            return 0
-
-        lax.fori_loop(0, buf.shape[2] // KC, chunk, 0)
+            twin_early_wait(p, yy)
+
+    def complete_late(p):
+        for yy in (left, right, far):
+            twin_wait(p, yy, False)
+
+    def complete(p, own_plane):
+        if own_plane:
+            for yy in (y, left, right, far):
+                twin_wait(p, yy, True)
+        else:
+            complete_early(p)
+            complete_late(p)
+
+    def product(p, r0, n, parts=((0, KC), (KC, KC))):
+        for k0, count in parts:
+            a = buf[pl.ds(p * 8, 8), :, k0:k0 + count].reshape(256, count)
+            part = lax.dot_general(wt[r0:r0 + n, k0:k0 + count], a, NT, preferred_element_type=F32)
+            res[r0:r0 + n] = part if k0 == 0 else res[r0:r0 + n] + part
 
     def span_of(p):
         return pl.ds(pl.multiple_of(p * 256, 256), 256)
@@ -285,12 +284,15 @@
                 for copy in halo_copies(i):
                     copy.start()
 
+    def store_first(p):
+        store_bc(p)
+        store_x(p)
+        send_halo(p)
+
     def project(p, own_plane):
         complete(p, own_plane)
         product(p, 0, FIRST)
-        store_bc(p)
-        store_x(p)
-        send_halo(p)
+        store_first(p)
 
     def gates(p):
         product(p, FIRST, W)
@@ -304,20 +306,23 @@
         q = (h + k + 1) % 4
         rcopy(taps.at[q], taps.at[q], cs.at[k], cr.at[q], head=h).wait_recv()
 
-    along(order[0], -1).start()
-    along(order[0], 1).start()
+    along(order[0], -1, True).start()
+    along(order[0], 1, True).start()
     begin(order[0], True)
-    for load in loads:
+    for load in smalls + loads:
         load.start()
-    taps[quarter, 0:4, 0:64] = cbc[...]
+    for load in smalls:
+        load.wait()
+    taps[quarter, 0:4, 0:64] = cbc_v[...]
     for k in range(3):
         taps_copy(k).start()
     wt[W + 64:FIRST, :] = jnp.concatenate(
-        [wdt[...].astype(F32), jnp.zeros((16 - HEADS, wt.shape[1]), F32)], axis=0).astype(BF16)
+        [wdt_v[...].astype(F32), jnp.zeros((16 - HEADS, wt.shape[1]), F32)], axis=0).astype(BF16)
     halo_x[...] = jnp.zeros_like(halo_x)
     halo_b[...] = jnp.zeros_like(halo_b)
     for load in loads:
         load.wait()
+    own.wait()
 
     arrive(1)
     near(order[0], True)
@@ -341,7 +346,11 @@
     last(order[3], False)
     pass_bc(order[1])
     pass_bc(order[2])
-    project(order[3], False)
+    complete_early(order[3])
+    product(order[3], 0, FIRST, ((0, EARLY),))
+    complete_late(order[3])
+    product(order[3], 0, FIRST, ((EARLY, buf.shape[2] - EARLY),))
+    store_first(order[3])
 
     def cols_of(b):
         return pl.ds(pl.multiple_of(slot_of(b // 2) * 256 + (b % 2) * 128, 128), 128)
@@ -368,8 +377,24 @@
     weight = step[...] * jnp.exp(tot - cum)
     cumt[...] = (cum - jnp.log(step[...])).T
 
+    def mate_totals():
+        return rcopy(tfin, tot_mate, ts, tr, seq=mate)
+
+    run_t = jnp.zeros((8, 128), F32)
+    first_t = run_t
+    for k in range(4):
+        if k:
+            first_t = jnp.where(first_run == k, run_t, first_t)
+            run_t = jnp.where(first_run == k, 0.0, run_t)
+        for b in (2 * k, 2 * k + 1):
+            offs[b] = run_t
+            run_t = run_t + tot[b * 8:(b + 1) * 8, :]
+    tfin[0] = jnp.where(first_run == 4, run_t, first_t)
+    tfin[1] = jnp.where(first_run == 4, 0.0, run_t)
+    mate_totals().start()
+
     lane = lax.broadcasted_iota(jnp.int32, (64, 128), 1)
-    tapx = jnp.concatenate([cx[...], jnp.zeros((4, W), F32)], axis=0).T
+    tapx = jnp.concatenate([cx_v[...], jnp.zeros((4, W), F32)], axis=0).T
 
     def conv_block(src, r0, taps, prev, b, dst, to):
         cur = src[r0:r0 + 64, cols_of(b)].astype(F32)
@@ -387,8 +412,8 @@
 
     for k in range(HEADS):
         conv(pre, k * 64, tapx[k * 64:(k + 1) * 64], xc)
+    pass_bc(order[3])
     gates(order[2])
-    pass_bc(order[3])
     for k in range(3):
         taps_wait(k)
     tapb = [taps[q].T[0:64] for q in range(4)]
@@ -425,55 +450,65 @@
         return jnp.concatenate(
             [jnp.broadcast_to(v[r + k:r + k + 1, :], (64, 128)) for k in range(HEADS)], axis=0)
 
-    def mate_copy(i):
-        return rcopy(sfin.at[i], st_mate.at[i], ss.at[i], sr.at[i], seq=mate)
-
-    def mate_total(i):
-        return rcopy(tfin.at[i], tot_mate.at[i], ts.at[i], tr.at[i], seq=mate)
-
     state = jnp.zeros((W, 128), F32)
-    total = jnp.zeros((8, 128), F32)
+    own_s[1] = state
     for k in range(4):
         if k:
             @pl.when(first_run == k)
             def _():
-                sfin[0] = state.astype(BF16)
-                tfin[0] = total
-                mate_copy(0).start()
-                mate_total(0).start()
+                own_s[0] = state
 
             state = jnp.where(first_run == k, 0.0, state)
-            total = jnp.where(first_run == k, 0.0, total)
         for b in (2 * k, 2 * k + 1):
             cols = slice(b * 128, (b + 1) * 128)
             sstart[b] = state
-            offs[b] = total
             xw = (xc[:, cols].astype(F32) * rows(weight, b * 8)).astype(BF16)
             fresh = lax.dot_general(xw, bcf[0:128, cols], NT, preferred_element_type=F32)
-            tb = tot[b * 8:(b + 1) * 8, :]
-            state = state * rows(jnp.exp(tb), 0) + fresh
-            total = total + tb
+            state = state * rows(jnp.exp(tot[b * 8:(b + 1) * 8, :]), 0) + fresh
 
     @pl.when(first_run == 4)
     def _():
-        sfin[0] = state.astype(BF16)
-        tfin[0] = total
-        mate_copy(0).start()
-        mate_total(0).start()
-        sfin[1] = jnp.zeros((W, 128), BF16)
-        tfin[1] = jnp.zeros((8, 128), F32)
+        own_s[0] = state
 
     @pl.when(first_run < 4)
     def _():
-        sfin[1] = state.astype(BF16)
-        tfin[1] = total
-
-    @pl.when(ends)
+        own_s[1] = state
+
+    def grown(v, t):
+        return v * rows(jnp.exp(t), 0)
+
+    mate_totals().wait_recv()
+    head_t = jnp.where(ends, tfin[0], tot_mate[0])
+    mid_t = jnp.where(ends, tot_mate[0], tfin[0])
+    tail_t = jnp.where(ends, tfin[1], tot_mate[1])
+    xfin[...] = (grown(own_s[0], jnp.where(ends, mid_t + tail_t, tail_t)) + own_s[1]).astype(BF16)
+    xtot[...] = head_t + mid_t + tail_t
+    for t in range(1, 4):
+        @pl.when(x + t < 4)
+        def _():
+            rcopy(xfin, st_in.at[x], xs.at[t], xr.at[x], seq=s + 2 * t).start()
+            rcopy(xtot, tot_in.at[x], vs.at[t], vr.at[x], seq=s + 2 * t).start()
+
+    def mate_copy(i):
+        return rcopy(sfin.at[i], st_mate.at[i], ss.at[i], sr.at[i], seq=mate)
+
+    @pl.when(middle)
     def _():
-        mate_copy(1).start()
-        mate_total(1).start()
+        sfin[0] = own_s[0].astype(BF16)
+        mate_copy(0).start()
 
     gates(order[3])
+    inc[0] = jnp.zeros((W, 128), F32)
+    for q in range(3):
+        @pl.when(q < x)
+        def _():
+            rcopy(xfin, st_in.at[q], xs.at[0], xr.at[q], seq=s).wait_recv()
+            rcopy(xtot, tot_in.at[q], vs.at[0], vr.at[q], seq=s).wait_recv()
+            inc[0] = grown(inc[0], tot_in[q]) + st_in[q].astype(F32)
+
+    carried = grown(inc[0], head_t)
+    sfin[1] = jnp.where(ends, carried + own_s[0], inc[0]).astype(BF16)
+    mate_copy(1).start()
     for b in range(8):
         cols = slice(b * 128, (b + 1) * 128)
         scores = lax.dot_general(bcf[0:128, cols], bcf[128:256, cols], TN, preferred_element_type=F32)
@@ -485,80 +520,45 @@
             yin[k * 64:(k + 1) * 64, cols] = jnp.dot(
                 xc[k * 64:(k + 1) * 64, cols], mixing.astype(BF16), preferred_element_type=F32)
 
-    mate_copy(0).wait_recv()
-    mate_total(0).wait_recv()
-
-    @pl.when(middle)
-    def _():
-        mate_copy(1).wait_recv()
-        mate_total(1).wait_recv()
-
-    def grown(v, t):
-        return v * rows(jnp.exp(t), 0)
-
-    head_s = jnp.where(ends, sfin[0].astype(F32), st_mate[0].astype(F32))
-    head_t = jnp.where(ends, tfin[0], tot_mate[0])
-    mid_s = jnp.where(ends, st_mate[0].astype(F32), sfin[0].astype(F32))
-    mid_t = jnp.where(ends, tot_mate[0], tfin[0])
-
-    @pl.when(middle)
-    def _():
-        tail_s[...] = st_mate[1].astype(F32)
-        tail_t[...] = tot_mate[1]
+    mate_copy(1).wait_recv()
+    met = st_mate[1].astype(F32)
+    inc[0] = jnp.where(ends, inc[0], carried) + met
 
     @pl.when(ends)
     def _():
-        tail_s[...] = sfin[1].astype(F32)
-        tail_t[...] = tfin[1]
-
-    xfin[...] = (grown(grown(head_s, mid_t) + mid_s, tail_t[...]) + tail_s[...]).astype(BF16)
-    xtot[...] = head_t + mid_t + tail_t[...]
-    for t in range(1, 4):
-        @pl.when(x + t < 4)
-        def _():
-            rcopy(xfin, st_in.at[x], xs.at[t], xr.at[x], seq=s + 2 * t).start()
-            rcopy(xtot, tot_in.at[x], vs.at[t], vr.at[x], seq=s + 2 * t).start()
-
-    inc[0] = jnp.zeros((W, 128), F32)
-    for q in range(3):
-        @pl.when(q < x)
-        def _():
-            rcopy(xfin, st_in.at[q], xs.at[0], xr.at[q], seq=s).wait_recv()
-            rcopy(xtot, tot_in.at[q], vs.at[0], vr.at[q], seq=s).wait_recv()
-            inc[0] = grown(inc[0], tot_in[q]) + st_in[q].astype(F32)
-
-    after_head = grown(inc[0], head_t) + head_s
-    inc[1] = grown(after_head, mid_t) + mid_s
-
-    @pl.when(middle)
-    def _():
-        inc[0] = after_head
+        mate_copy(0).wait_recv()
+        inc[1] = grown(grown(inc[0], head_t) + own_s[0], mid_t) + st_mate[0].astype(F32)
 
     skips = jnp.concatenate([jnp.full((64, 128), skip[k], F32) for k in range(HEADS)], axis=0)
-    for b in range(8):
-        cols = slice(b * 128, (b + 1) * 128)
-        run = jnp.where(first_run <= b // 2, 1, 0)
-        st = (sstart[b] + inc[run] * rows(jnp.exp(offs[b]), 0)).astype(BF16)
-        yst = jnp.dot(st, bcf[128:256, cols], preferred_element_type=F32)
-        yv = yin[:, cols] + yst * rows(jnp.exp(cums[b * 8:(b + 1) * 8, :]), 0) + skips * xc[:, cols].astype(F32)
-        yv = yv.astype(BF16).astype(F32)
-        g = (yv * silu(pre[W:BB, cols_of(b)].astype(F32))).T
-        for i in range(4):
-            dst = slot_of(b // 2) * 8 + 4 * (b % 2) + i
-            sb[dst, :, 0:W] = g[32 * i:32 * i + 16, :].astype(BF16)
-            sb[dst, :, W:BB] = g[32 * i + 16:32 * i + 32, :].astype(BF16)
-
-    def scatter(k, _):
-        dst = (h + 16 + k) % 32
-
-        @pl.when(k != 16)
-        def _():
-            rcopy(sb.at[dst], rbuf.at[h], as_.at[dst], ar.at[h], seq=owner(dst // 8), head=dst).start()
-
-        return 0
-
-    lax.fori_loop(0, 32, scatter, 0)
-    rbuf[h] = sb[h]
+    def send_out(dst):
+        return rcopy(sb.at[dst], rbuf.at[h], as_.at[dst], ar.at[h], seq=owner(dst // 8), head=dst)
+
+    for slot in (order[3], order[1], order[2], order[0]):
+        for half in range(2):
+            k = (slot - turn + 4) % 4
+            b = 2 * k + half
+            cols = pl.ds(pl.multiple_of(b * 128, 128), 128)
+            run = jnp.where(first_run <= k, 1, 0)
+            st = (sstart[b] + inc[run] * rows(jnp.exp(offs[b]), 0)).astype(BF16)
+            yst = jnp.dot(st, bcf[128:256, cols], preferred_element_type=F32)
+            near_t = jnp.exp(cums[pl.ds(pl.multiple_of(b * 8, 8), 8), :])
+            yv = yin[:, cols] + yst * rows(near_t, 0) + skips * xc[:, cols].astype(F32)
+            yv = yv.astype(BF16).astype(F32)
+            gate = pre[W:BB, pl.ds(pl.multiple_of(slot * 256 + half * 128, 128), 128)]
+            g = (yv * silu(gate.astype(F32))).T
+            for i in range(4):
+                dst = slot * 8 + 4 * half + i
+                sb[dst, :, 0:W] = g[32 * i:32 * i + 16, :].astype(BF16)
+                sb[dst, :, W:BB] = g[32 * i + 16:32 * i + 32, :].astype(BF16)
+            for i in range(4):
+                dst = slot * 8 + 4 * half + i
+
+                @pl.when(dst != h)
+                def _():
+                    send_out(dst).start()
+
+    keep = pltpu.make_async_copy(sb.at[h], rbuf.at[h], lsem.at[7])
+    keep.start()
 
     def collect(k, _):
         src = (h + k) % 32
@@ -567,9 +567,56 @@
 
     lax.fori_loop(1, 32, collect, 0)
 
+    keep.wait()
+    for k in range(3):
+        taps_copy(k).wait_send()
+    for j in range(4):
+        p = order[j]
+        for sign in (-1, 1)[:2 if j == 0 else 1 if j == 1 else 0]:
+            along(p, sign, j == 0).wait_send()
+            for yy in (left, right, far):
+                along_early(p, yy, sign).wait_send()
+        for kind in range(4):
+            ring(p, kind, j == 0).wait_send()
+        twin(p, y, True, j == 0).wait_send()
+        for yy in (left, right, far):
+            twin(p, yy, j == 0).wait_send()
+            if j:
+                twin_early(p, yy).wait_send()
+        for kind in range(3):
+            share_copy(p, kind).wait_send()
+
+    for i in range(2):
+        @pl.when(halo_when[i])
+        def _():
+            for copy in halo_copies(i):
+                copy.wait_send()
+
+    mate_totals().wait_send()
+    mate_copy(1).wait_send()
+
+    @pl.when(middle)
+    def _():
+        mate_copy(0).wait_send()
+
+    for t in range(1, 4):
+        @pl.when(x + t < 4)
+        def _():
+            rcopy(xfin, st_in.at[x], xs.at[t], xr.at[x], seq=s).wait_send()
+            rcopy(xtot, tot_in.at[x], vs.at[t], vr.at[x], seq=s).wait_send()
+
+    def sent(k, _):
+        dst = (h + k) % 32
+        rcopy(sb.at[dst], rbuf.at[h], as_.at[dst], ar.at[h], head=h).wait_send()
+        return 0
+
+    lax.fori_loop(1, 32, sent, 0)
+
+
+def norm_kernel(parts, gain, out, asm):
     for q in range(32):
-        asm[0:16, q * W:(q + 1) * W] = rbuf[q, :, 0:W]
-        asm[16:32, q * W:(q + 1) * W] = rbuf[q, :, W:BB]
+        asm[0:16, q * W:(q + 1) * W] = parts[q, :, 0:W]
+        asm[16:32, q * W:(q + 1) * W] = parts[q, :, W:BB]
     for g in range(5):
         v = asm[:, g * 2048:(g + 1) * 2048].astype(F32)
         scale = lax.rsqrt(jnp.mean(v * v, axis=1, keepdims=True) + 1e-5)
@@ -578,51 +625,6 @@
             out[:, c0 * 128:(c0 + 1) * 128] = (
                 v[:, k * 128:(k + 1) * 128] * scale * gain[c0:c0 + 1, :]).astype(BF16)
 
-    for k in range(3):
-        taps_copy(k).wait_send()
-    for j in range(4):
-        p = order[j]
-        for sign in (-1, 1)[:2 if j == 0 else 1 if j == 1 else 0]:
-            along(p, sign).wait_send()
-            for yy in (left, right, far):
-                along_early(p, yy, sign).wait_send()
-        for kind in range(4):
-            ring(p, kind, j == 0).wait_send()
-        twin(p, y, True).wait_send()
-        for yy in (left, right, far):
-            twin(p, yy, j == 0).wait_send()
-            if j:
-                twin_early(p, yy).wait_send()
-        for kind in range(3):
-            share_copy(p, kind).wait_send()
-
-    for i in range(2):
-        @pl.when(halo_when[i])
-        def _():
-            for copy in halo_copies(i):
-                copy.wait_send()
-
-    mate_copy(0).wait_send()
-    mate_total(0).wait_send()
-
-    @pl.when(ends)
-    def _():
-        mate_copy(1).wait_send()
-        mate_total(1).wait_send()
-
-    for t in range(1, 4):
-        @pl.when(x + t < 4)
-        def _():
-            rcopy(xfin, st_in.at[x], xs.at[t], xr.at[x], seq=s).wait_send()
-            rcopy(xtot, tot_in.at[x], vs.at[t], vr.at[x], seq=s).wait_send()
-
-    def sent(k, _):
-        dst = (h + k) % 32
-        rcopy(sb.at[dst], rbuf.at[h], as_.at[dst], ar.at[h], head=h).wait_send()
-        return 0
-
-    lax.fori_loop(1, 32, sent, 0)
-
 
 def call(tok, wx, wz, wbc, wdt, cx, cbc, bias, alog, skip, gain):
     d = tok.shape[1]
@@ -631,32 +633,41 @@
     sm = pl.BlockSpec(memory_space=pltpu.SMEM)
     dma = pltpu.SemaphoreType.DMA
     mem = pltpu.VMEM
-    return pl.pallas_call(
+    parts = pl.pallas_call(
         kernel,
-        out_shape=jax.ShapeDtypeStruct((32, 10240), BF16),
-        in_specs=[anywhere] * 4 + [vm] * 3 + [sm] * 3 + [vm],
-        out_specs=vm,
+        out_shape=jax.ShapeDtypeStruct((32, 16, BB), BF16),
+        in_specs=[anywhere] * 7 + [sm] * 3,
+        out_specs=anywhere,
         scratch_shapes=[
+            mem((HEADS, d), BF16), mem((4, W), F32), mem((4, 64), F32),
             mem((32, 32, d), BF16), mem((BB + 80, d), BF16), mem((BB + 80, 256), F32),
             mem((BB, 1024), BF16), mem((16, 1024), F32), mem((256, 1024), BF16), mem((256, 1024), BF16),
             mem((2, 16, 384), BF16), mem((2, 16, 128), BF16), mem((2, 16, 384), BF16), mem((2, 4, 16, 128), BF16),
             mem((2, W + 256, 128), F32), mem((4, 8, 128), F32), mem((W, 1024), BF16),
             mem((64, 128), F32), mem((64, 128), F32), mem((128, 64), F32), mem((W, 1024), F32),
             mem((8, W, 128), F32), mem((8, 8, 128), F32), mem((2, W, 128), BF16), mem((2, 8, 128), F32),
-            mem((2, W, 128), BF16), mem((2, 8, 128), F32), mem((W, 128), F32), mem((8, 128), F32),
+            mem((2, W, 128), BF16), mem((2, 8, 128), F32), mem((2, W, 128), F32),
             mem((W, 128), BF16), mem((8, 128), F32),
             mem((3, W, 128), BF16), mem((3, 8, 128), F32), mem((2, W, 128), F32),
-            mem((32, 16, BB), BF16), mem((32, 16, BB), BF16), mem((32, 10240), BF16),
-            dma((4,)), dma((4, 2)), dma((4,)), dma((4, 4, 2)), dma((4, 4)),
+            mem((32, 16, BB), BF16),
+            dma((8,)), dma((4, 2)), dma((4,)), dma((4, 4, 2)), dma((4, 4)),
             dma((4, 4)), dma((4, 4)), dma((4, 4)), dma((4, 4)), dma((4, 4)), dma((4, 4)),
             dma((4, 3)), dma((4, 3)), dma((3,)), dma((4,)), dma((2,)), dma((2,)), dma((2, 4)), dma((2, 4)),
-            dma((2,)), dma((2,)), dma((2,)), dma((2,)), dma((4,)), dma((3,)), dma((4,)), dma((3,)),
+            dma((2,)), dma((2,)), dma, dma, dma((4,)), dma((3,)), dma((4,)), dma((3,)),
             dma((32,)), dma((32,)),
         ],
         compiler_params=pltpu.CompilerParams(collective_id=0, has_side_effects=True,
                                              vmem_limit_bytes=60 * 2**20),
         name="mixer",
-    )(tok, wx, wz, wbc, wdt, cx, cbc, bias, alog, skip, gain.reshape(80, 128))
+    )(tok, wx, wz, wbc, wdt, cx, cbc, bias, alog, skip)
+    return pl.pallas_call(
+        norm_kernel,
+        out_shape=jax.ShapeDtypeStruct((32, 10240), BF16),
+        in_specs=[vm, vm],
+        out_specs=vm,
+        scratch_shapes=[mem((32, 10240), BF16)],
+        name="norm",
+    )(parts, gain.reshape(80, 128))
 
 
 def shards(tokens, wx, wz, wbc, wdt, cx, cbc, bias, alog, skip, gain):

time: 110 us -> 106 us (0.964)
  Pallas kernels: 108 us -> 106 us
  local copies, waits for them, and re-layouts: 1.97 us -> 0 us
    pallas_call x1 -> x2, Pallas kernels: 108 us -> 106 us  [the longest x1 104 us: call(): pl.pallas_call(kernel, out_shape=jax.ShapeDtypeStruct((32, 16, BB), BF16)...]
    unnamed x1 -> x0, local copies, waits for them, and re-layouts: 1.97 us -> none
where the time goes in v4:
time: 106 us
  Pallas kernels  106 us (100%)
    pallas_call x1, Pallas kernels, call(): pl.pallas_call(kernel, out_shape=jax.ShapeDtypeStruct((32, 16, BB), BF16)...  104 us
    pallas_call x1, Pallas kernels, call(): pl.pallas_call(norm_kernel, out_shape=jax.ShapeDtypeStruct((32, 10240), B...  2.36 us

profile of v4, /device:TPU:7, one launch (start us, length us, event | category | flops | bytes accessed | tf_op | source)
XLA Modules:
  0.0 105.9 jit_solution(2811035139223924199)
XLA Ops:
  0.0 103.5 %mixer.1.parts = bf16[32,16,640]{2,1,0:T(8,128)(2,1)} custom-call(bf16[32,8192]{1,0:T(8,128)(2,1)} %tok.1, bf16[320,8192]{1,0:T(8,128)(2,1)} %bitcast.5, bf16[320,8192]{1,0:T(8,128)(2,1)} %bitcast.6, bf16[64,8192]{1,0:T(8,128)(2,1)} %bitcast.7, bf16[5,8192]{1,0:T(8,128)(2,1)} %bitcast.8, f32[4,320]{1,0:T(4,128)} %cx.1, f32[4,64]{1,0:T(4,128)} %cbc.1, ...), custom_call_target="tpu_custom_call" | custom-call | tf_op jit(solution)/shard_map/mixer/pallas_call | solution.py:636
  103.5 2.4 %norm.1 = bf16[32,10240]{1,0:T(8,128)(2,1)} custom-call(bf16[32,16,640]{2,1,0:T(8,128)(2,1)} %mixer.1.parts, f32[80,128]{1,0:T(8,128)} %bitcast.9), custom_call_target="tpu_custom_call" | custom-call | tf_op jit(solution)/shard_map/norm/pallas_call | solution.py:663

commit v5 on v4

--- a/solution.py
+++ b/solution.py
@@ -82,17 +82,17 @@
     def signal(**device):
         pl.semaphore_signal(barrier, inc=1, device_id=device, device_id_type=MESH)
 
-    def greet(k, _):
-        there = (place + 6 + k // 8) % 8
-        who = (there % 4) * 8 + k % 8
-
-        @pl.when(k != 16 + h % 8)
-        def _():
-            signal(seq=x * 2 + there // 4, head=who)
-
-        return 0
-
-    lax.fori_loop(0, 32, greet, 0)
+    for dz in (-1, 1, -2, 0):
+        there = (place + dz + 8) % 8
+        seq, first = x * 2 + there // 4, (there % 4) * 8
+        for k in range(8):
+            if dz:
+                signal(seq=seq, head=first + k)
+            else:
+                @pl.when(first + k != h)
+                def _():
+                    signal(seq=seq, head=first + k)
+
     for k in range(1, 4):
         signal(seq=(s + 2 * k) % NSEQ)
     for k in range(4):
@@ -520,6 +520,43 @@
             yin[k * 64:(k + 1) * 64, cols] = jnp.dot(
                 xc[k * 64:(k + 1) * 64, cols], mixing.astype(BF16), preferred_element_type=F32)
 
+    for k in range(3):
+        taps_copy(k).wait_send()
+    for j in range(4):
+        p = order[j]
+        for sign in (-1, 1)[:2 if j == 0 else 1 if j == 1 else 0]:
+            along(p, sign, j == 0).wait_send()
+            for yy in (left, right, far):
+                along_early(p, yy, sign).wait_send()
+        for kind in range(4):
+            ring(p, kind, j == 0).wait_send()
+        twin(p, y, True, j == 0).wait_send()
+        for yy in (left, right, far):
+            twin(p, yy, j == 0).wait_send()
+            if j:
+                twin_early(p, yy).wait_send()
+        for kind in range(3):
+            share_copy(p, kind).wait_send()
+
+    for i in range(2):
+        @pl.when(halo_when[i])
+        def _():
+            for copy in halo_copies(i):
+                copy.wait_send()
+
+    mate_totals().wait_send()
+    mate_copy(1).wait_send()
+
+    @pl.when(middle)
+    def _():
+        mate_copy(0).wait_send()
+
+    for t in range(1, 4):
+        @pl.when(x + t < 4)
+        def _():
+            rcopy(xfin, st_in.at[x], xs.at[t], xr.at[x], seq=s).wait_send()
+            rcopy(xtot, tot_in.at[x], vs.at[t], vr.at[x], seq=s).wait_send()
+
     mate_copy(1).wait_recv()
     met = st_mate[1].astype(F32)
     inc[0] = jnp.where(ends, inc[0], carried) + met
@@ -531,7 +568,7 @@
 
     skips = jnp.concatenate([jnp.full((64, 128), skip[k], F32) for k in range(HEADS)], axis=0)
     def send_out(dst):
-        return rcopy(sb.at[dst], rbuf.at[h], as_.at[dst], ar.at[h], seq=owner(dst // 8), head=dst)
+        return rcopy(sb.at[dst], rbuf.at[h], as_, ar, seq=owner(dst // 8), head=dst)
 
     for slot in (order[3], order[1], order[2], order[0]):
         for half in range(2):
@@ -560,57 +597,10 @@
     keep = pltpu.make_async_copy(sb.at[h], rbuf.at[h], lsem.at[7])
     keep.start()
 
-    def collect(k, _):
-        src = (h + k) % 32
-        rcopy(sb.at[src], rbuf.at[src], as_.at[src], ar.at[src], head=h).wait_recv()
-        return 0
-
-    lax.fori_loop(1, 32, collect, 0)
-
+    everyone = rcopy(sb.at[pl.ds(0, 31)], rbuf.at[pl.ds(0, 31)], as_, ar, head=h)
+    everyone.wait_send()
+    everyone.wait_recv()
     keep.wait()
-    for k in range(3):
-        taps_copy(k).wait_send()
-    for j in range(4):
-        p = order[j]
-        for sign in (-1, 1)[:2 if j == 0 else 1 if j == 1 else 0]:
-            along(p, sign, j == 0).wait_send()
-            for yy in (left, right, far):
-                along_early(p, yy, sign).wait_send()
-        for kind in range(4):
-            ring(p, kind, j == 0).wait_send()
-        twin(p, y, True, j == 0).wait_send()
-        for yy in (left, right, far):
-            twin(p, yy, j == 0).wait_send()
-            if j:
-                twin_early(p, yy).wait_send()
-        for kind in range(3):
-            share_copy(p, kind).wait_send()
-
-    for i in range(2):
-        @pl.when(halo_when[i])
-        def _():
-            for copy in halo_copies(i):
-                copy.wait_send()
-
-    mate_totals().wait_send()
-    mate_copy(1).wait_send()
-
-    @pl.when(middle)
-    def _():
-        mate_copy(0).wait_send()
-
-    for t in range(1, 4):
-        @pl.when(x + t < 4)
-        def _():
-            rcopy(xfin, st_in.at[x], xs.at[t], xr.at[x], seq=s).wait_send()
-            rcopy(xtot, tot_in.at[x], vs.at[t], vr.at[x], seq=s).wait_send()
-
-    def sent(k, _):
-        dst = (h + k) % 32
-        rcopy(sb.at[dst], rbuf.at[h], as_.at[dst], ar.at[h], head=h).wait_send()
-        return 0
-
-    lax.fori_loop(1, 32, sent, 0)
 
 
 def norm_kernel(parts, gain, out, asm):
@@ -654,7 +644,7 @@
             dma((4, 4)), dma((4, 4)), dma((4, 4)), dma((4, 4)), dma((4, 4)), dma((4, 4)),
             dma((4, 3)), dma((4, 3)), dma((3,)), dma((4,)), dma((2,)), dma((2,)), dma((2, 4)), dma((2, 4)),
             dma((2,)), dma((2,)), dma, dma, dma((4,)), dma((3,)), dma((4,)), dma((3,)),
-            dma((32,)), dma((32,)),
+            dma, dma,
         ],
         compiler_params=pltpu.CompilerParams(collective_id=0, has_side_effects=True,
                                              vmem_limit_bytes=60 * 2**20),

time: 106 us -> 105 us (level)
  Pallas kernels: 106 us -> 104 us
    pallas_call x1, Pallas kernels: 104 us -> 102 us  [call(): pl.pallas_call(kernel, out_shape=jax.ShapeDtypeStruct((32, 16, BB), BF16)...]
where the time goes in v5:
time: 105 us; the launch traced here: 104 us
  Pallas kernels  104 us (99%)
    pallas_call x1, Pallas kernels, call(): pl.pallas_call(kernel, out_shape=jax.ShapeDtypeStruct((32, 16, BB), BF16)...  102 us
    pallas_call x1, Pallas kernels, call(): pl.pallas_call(norm_kernel, out_shape=jax.ShapeDtypeStruct((32, 10240), B...  2.36 us

profile of v5, /device:TPU:7, one launch (start us, length us, event | category | flops | bytes accessed | tf_op | source)
XLA Modules:
  0.0 104.2 jit_solution(15301093594861379066)
XLA Ops:
  0.0 101.8 %mixer.1.parts = bf16[32,16,640]{2,1,0:T(8,128)(2,1)} custom-call(bf16[32,8192]{1,0:T(8,128)(2,1)} %tok.1, bf16[320,8192]{1,0:T(8,128)(2,1)} %bitcast.5, bf16[320,8192]{1,0:T(8,128)(2,1)} %bitcast.6, bf16[64,8192]{1,0:T(8,128)(2,1)} %bitcast.7, bf16[5,8192]{1,0:T(8,128)(2,1)} %bitcast.8, f32[4,320]{1,0:T(4,128)} %cx.1, f32[4,64]{1,0:T(4,128)} %cbc.1, ...), custom_call_target="tpu_custom_call" | custom-call | tf_op jit(solution)/shard_map/mixer/pallas_call | solution.py:626
  101.8 2.4 %norm.1 = bf16[32,10240]{1,0:T(8,128)(2,1)} custom-call(bf16[32,16,640]{2,1,0:T(8,128)(2,1)} %mixer.1.parts, f32[80,128]{1,0:T(8,128)} %bitcast.9), custom_call_target="tpu_custom_call" | custom-call | tf_op jit(solution)/shard_map/norm/pallas_call | solution.py:653

commit v6 on v5

--- a/solution.py
+++ b/solution.py
@@ -603,17 +603,28 @@
     keep.wait()
 
 
-def norm_kernel(parts, gain, out, asm):
-    for q in range(32):
-        asm[0:16, q * W:(q + 1) * W] = parts[q, :, 0:W]
-        asm[16:32, q * W:(q + 1) * W] = parts[q, :, W:BB]
-    for g in range(5):
-        v = asm[:, g * 2048:(g + 1) * 2048].astype(F32)
-        scale = lax.rsqrt(jnp.mean(v * v, axis=1, keepdims=True) + 1e-5)
-        for k in range(16):
-            c0 = g * 16 + k
-            out[:, c0 * 128:(c0 + 1) * 128] = (
-                v[:, k * 128:(k + 1) * 128] * scale * gain[c0:c0 + 1, :]).astype(BF16)
+def norm_kernel(parts, gain, out, held, asm, done, sems):
+    loads = [pltpu.make_async_copy(parts.at[pl.ds(8 * i, 8)], held.at[pl.ds(8 * i, 8)], sems.at[i])
+             for i in range(4)]
+    stores = [pltpu.make_async_copy(done.at[:, pl.ds(g * 2048, 2048)], out.at[:, pl.ds(g * 2048, 2048)],
+                                    sems.at[4 + g]) for g in range(5)]
+    for load in loads:
+        load.start()
+    for i, groups in enumerate(((0,), (1,), (2,), (3, 4))):
+        loads[i].wait()
+        for q in range(8 * i, 8 * i + 8):
+            asm[0:16, q * W:(q + 1) * W] = held[q, :, 0:W]
+            asm[16:32, q * W:(q + 1) * W] = held[q, :, W:BB]
+        for g in groups:
+            v = asm[:, g * 2048:(g + 1) * 2048].astype(F32)
+            scale = lax.rsqrt(jnp.mean(v * v, axis=1, keepdims=True) + 1e-5)
+            for k in range(16):
+                c0 = g * 16 + k
+                done[:, c0 * 128:(c0 + 1) * 128] = (
+                    v[:, k * 128:(k + 1) * 128] * scale * gain[c0:c0 + 1, :]).astype(BF16)
+            stores[g].start()
+    for store in stores:
+        store.wait()
 
 
 def call(tok, wx, wz, wbc, wdt, cx, cbc, bias, alog, skip, gain):
@@ -653,9 +664,9 @@
     return pl.pallas_call(
         norm_kernel,
         out_shape=jax.ShapeDtypeStruct((32, 10240), BF16),
-        in_specs=[vm, vm],
-        out_specs=vm,
-        scratch_shapes=[mem((32, 10240), BF16)],
+        in_specs=[anywhere, vm],
+        out_specs=anywhere,
+        scratch_shapes=[mem((32, 16, BB), BF16), mem((32, 10240), BF16), mem((32, 10240), BF16), dma((9,))],
         name="norm",
     )(parts, gain.reshape(80, 128))
 

time: 105 us -> 106 us (level)
  no operation moved by 1% of the time
where the time goes in v6:
time: 106 us; the launch traced here: 105 us
  Pallas kernels  105 us (99%)
    pallas_call x1, Pallas kernels, call(): pl.pallas_call(kernel, out_shape=jax.ShapeDtypeStruct((32, 16, BB), BF16)...  102 us
    pallas_call x1, Pallas kernels, call(): pl.pallas_call(norm_kernel, out_shape=jax.ShapeDtypeStruct((32, 10240), B...  3.35 us

profile of v6, /device:TPU:7, one launch (start us, length us, event | category | flops | bytes accessed | tf_op | source)
XLA Modules:
  0.0 105.3 jit_solution(1802407017473633915)
XLA Ops:
  0.0 101.8 %mixer.1.parts = bf16[32,16,640]{2,1,0:T(8,128)(2,1)} custom-call(bf16[32,8192]{1,0:T(8,128)(2,1)} %tok.1, bf16[320,8192]{1,0:T(8,128)(2,1)} %bitcast.5, bf16[320,8192]{1,0:T(8,128)(2,1)} %bitcast.6, bf16[64,8192]{1,0:T(8,128)(2,1)} %bitcast.7, bf16[5,8192]{1,0:T(8,128)(2,1)} %bitcast.8, f32[4,320]{1,0:T(4,128)} %cx.1, f32[4,64]{1,0:T(4,128)} %cbc.1, ...), custom_call_target="tpu_custom_call" | custom-call | tf_op jit(solution)/shard_map/mixer/pallas_call | solution.py:637
  101.8 3.3 %norm.1 = bf16[32,10240]{1,0:T(8,128)(2,1)} custom-call(bf16[32,16,640]{2,1,0:T(8,128)(2,1)} %mixer.1.parts, f32[80,128]{1,0:T(8,128)} %bitcast.9), custom_call_target="tpu_custom_call" | custom-call | tf_op jit(solution)/shard_map/norm/pallas_call | solution.py:664
